TPU v7x, 1024 devices: a whole 4x4x32 slice. The times are simulated.
1024 devices in a mesh: blk: 64 (over y, x, z_hi), grp: 16 (over z_lo, core).
Axes of the slice: x: 4, y: 4, z: 32 (z_hi: 4, z_lo: 8; z = z_hi * 8 + z_lo), core: 2. Of those that a mesh axis runs over, the one named last changes fastest.
Arguments:
- image_embed: bfloat16 [262144, 1152], P(('blk', 'grp')), may hold values from -0.19921875 to 0.19921875
- text_embed: bfloat16 [262144, 1152], P(('blk', 'grp')), may hold values from -0.19921875 to 0.19921875
- log_temp: float32 [1], replicated, may hold values from 1.4 to 2.1
- logit_bias: float32 [1], replicated, may hold values from -5 to -3
Outputs:
- loss_rows: float32 [262144], P(('blk', 'grp'))
- grad_image: bfloat16 [262144, 1152], P(('blk', 'grp'))
- grad_text: bfloat16 [262144, 1152], P(('blk', 'grp'))
All inputs are finite; a program needn't handle non-finite values.
Results may differ from a plain program's by a relative error of at most 0.0054.
Values may be sent and summed in bfloat16 or wider, within the bound.
No kernel may reach another device: no remote copies, remote signals or barrier semaphores. Data moves between devices by JAX's collectives and lax.ppermute only.
A program may use at most 32 MiB of HBM per device.

v0:
```python
import jax
import jax.numpy as jnp
from jax import lax
from jax.sharding import PartitionSpec as P

SHIFTS = 2


def from_behind(block, axis, distance):
    devices = range(lax.axis_size(axis))
    route = [((i - distance) % len(devices), i) for i in devices]
    return lax.ppermute(block, axis, route)


def normalize(embed):
    wide = embed.astype(jnp.float32)
    inv = 1.0 / jnp.sqrt(jnp.sum(wide * wide, axis=-1, keepdims=True) + 1e-06)
    unit = wide * inv
    return (inv, unit, unit.astype(jnp.bfloat16))


def unnormalize(inv, unit, grad):
    return (inv * (grad - unit * jnp.sum(unit * grad, axis=-1, keepdims=True))).astype(jnp.bfloat16)


def text_step(block, offset):
    return from_behind(block, "blk", offset)


def send_home(term, offset):
    return from_behind(term, "blk", offset)


def on_device(image_embed, text_embed, log_temp, logit_bias):
    rows = image_embed.shape[0]
    inv_img, unit_img, img_hat = normalize(image_embed)
    inv_txt, unit_txt, txt_hat = normalize(text_embed)
    scale = jnp.exp(log_temp[0])
    eye = jnp.eye(rows, dtype=jnp.float32)
    blocks = {0: txt_hat}
    upward = txt_hat
    downward = txt_hat
    for step in range(1, SHIFTS + 1):
        upward = text_step(upward, -1)
        downward = text_step(downward, 1)
        blocks[step] = upward
        blocks[-step] = downward
    loss = jnp.zeros((rows,), jnp.float32)
    d_img = jnp.zeros(image_embed.shape, jnp.float32)
    terms = {}
    for s in range(-SHIFTS, SHIFTS + 1):
        other = blocks[s]
        logits = (
            scale * jnp.dot(img_hat, other.T, preferred_element_type=jnp.float32) + logit_bias[0]
        )
        if s == 0:
            sign = 2.0 * eye - 1.0
            target = eye
        else:
            sign = -jnp.ones_like(eye)
            target = jnp.zeros_like(eye)
        loss = loss + jnp.sum(jax.nn.softplus(-sign * logits), axis=-1)
        weights = (jax.nn.sigmoid(logits) - target).astype(jnp.bfloat16)
        d_img = d_img + scale * jnp.dot(weights, other, preferred_element_type=jnp.float32)
        terms[s] = scale * jnp.dot(weights.T, img_hat, preferred_element_type=jnp.float32)
    d_txt = terms[0]
    for s in range(1, SHIFTS + 1):
        d_txt = d_txt + send_home(terms[s], s) + send_home(terms[-s], -s)
    grad_image = unnormalize(inv_img, unit_img, d_img)
    grad_text = unnormalize(inv_txt, unit_txt, d_txt)
    return (loss, grad_image, grad_text)


def solution(mesh):
    in_specs = (P(("blk", "grp"), None), P(("blk", "grp"), None), P(), P())
    out_specs = (P(("blk", "grp")), P(("blk", "grp"), None), P(("blk", "grp"), None))
    return jax.shard_map(
        on_device, mesh=mesh, in_specs=in_specs, out_specs=out_specs, check_vma=False
    )
```

profile of v0, /device:TPU:200, one launch (start us, length us, event | category | flops | bytes accessed | tf_op | source)
XLA Modules:
  0.0 1020.6 jit_solution(11007044948359920210)
XLA Ops:
  0.6 0.0 copy-start
  0.6 1.3 fusion.21
  2.0 1.2 fusion.8
  3.2 18.5 %collective-permute-start.2 = (bf16[256,1152]{1,0:T(8,128)(2,1)S(1)}, bf16[256,1152]{1,0:T(8,128)(2,1)S(1)}, u32[]{:S(2)}, u32[]{:S(2)}) collective-permute-start(bf16[256,1152]{1,0:T(8,128)(2,1)S(1)} %fusion.8), channel_id=1, source_target_pairs={{16,0},{32,16},{48,32},{64,48},{80,64},{96,80},{112,96},{128,112},... | collective-permute-start | bytes 1769480 | tf_op jit(solution)/shard_map/ppermute | solution.py:12
  21.7 1.9 collective-permute-start
  23.6 0.0 copy-done
  23.6 0.2 fusion.16
  25.2 0.6 fusion.29
  25.8 0.4 fusion.33
  26.2 113.8 %collective-permute-done = bf16[256,1152]{1,0:T(8,128)(2,1)S(1)} collective-permute-done((bf16[256,1152]{1,0:T(8,128)(2,1)S(1)}, bf16[256,1152]{1,0:T(8,128)(2,1)S(1)}, u32[]{:S(2)}, u32[]{:S(2)}) %collective-permute-start) | collective-permute-done | bytes 589856 | tf_op jit(solution)/shard_map/ppermute | solution.py:12
  140.0 0.6 fusion.28
  140.6 0.4 convolution_multiply_fusion.2
  141.1 5.7 collective-permute-start.5
  146.8 8.9 collective-permute-start.1
  155.7 171.3 %collective-permute-done.2 = bf16[256,1152]{1,0:T(8,128)(2,1)S(1)} collective-permute-done((bf16[256,1152]{1,0:T(8,128)(2,1)S(1)}, bf16[256,1152]{1,0:T(8,128)(2,1)S(1)}, u32[]{:S(2)}, u32[]{:S(2)}) %collective-permute-start.2) | collective-permute-done | bytes 589856 | tf_op jit(solution)/shard_map/ppermute | solution.py:12
  327.0 0.6 fusion.30
  327.6 0.4 convolution_multiply_fusion.3
  328.0 1.9 collective-permute-start.4
  329.9 17.1 %collective-permute-start.3 = (bf16[256,1152]{1,0:T(8,128)(2,1)S(1)}, bf16[256,1152]{1,0:T(8,128)(2,1)S(1)}, u32[]{:S(2)}, u32[]{:S(2)}) collective-permute-start(bf16[256,1152]{1,0:T(8,128)(2,1)S(1)} %collective-permute-done.2), channel_id=1, source_target_pairs={{16,0},{32,16},{48,32},{64,48},{80,64},{96,80},{112,96},{128,112},... | collective-permute-start | bytes 1769480 | tf_op jit(solution)/shard_map/ppermute | solution.py:12
  347.0 0.4 fusion.32
  347.4 91.7 %collective-permute-done.1 = bf16[256,1152]{1,0:T(8,128)(2,1)S(1)} collective-permute-done((bf16[256,1152]{1,0:T(8,128)(2,1)S(1)}, bf16[256,1152]{1,0:T(8,128)(2,1)S(1)}, u32[]{:S(2)}, u32[]{:S(2)}) %collective-permute-start.1) | collective-permute-done | bytes 589856 | tf_op jit(solution)/shard_map/ppermute | solution.py:12
  439.2 0.6 fusion.27
  439.7 0.4 convolution_multiply_fusion
  440.2 2.3 collective-permute-start.7
  442.5 378.9 %collective-permute-done.3 = bf16[256,1152]{1,0:T(8,128)(2,1)S(1)} collective-permute-done((bf16[256,1152]{1,0:T(8,128)(2,1)S(1)}, bf16[256,1152]{1,0:T(8,128)(2,1)S(1)}, u32[]{:S(2)}, u32[]{:S(2)}) %collective-permute-start.3) | collective-permute-done | bytes 589856 | tf_op jit(solution)/shard_map/ppermute | solution.py:12
  821.3 0.6 fusion.31
  821.9 0.4 convolution_multiply_fusion.1
  822.4 1.9 collective-permute-start.6
  824.3 0.6 add_add_fusion
  824.9 0.4 fusion
  825.3 0.4 convolution_add_fusion.1
  825.7 0.5 fusion.12
  826.2 0.0 copy-start.1
  826.2 1.1 fusion.15
  827.3 0.0 collective-permute-done.5
  827.3 0.0 collective-permute-done.4
  827.3 0.0 collective-permute-done.7
  827.3 191.4 %collective-permute-done.6 = f32[256,1152]{1,0:T(8,128)S(1)} collective-permute-done((f32[256,1152]{1,0:T(8,128)S(1)}, f32[256,1152]{1,0:T(8,128)S(1)}, u32[]{:S(2)}, u32[]{:S(2)}) %collective-permute-start.6) | collective-permute-done | bytes 1179680 | tf_op jit(solution)/shard_map/ppermute | solution.py:12
  1018.7 0.0 copy-done.1
  1018.7 0.8 fusion.17
  1019.5 1.1 fusion.20
  (2 shorter events, 0.0 us)
Async XLA Ops:
  0.6 23.0 %copy-start = (bf16[256,1152]{1,0:T(8,128)(2,1)S(1)}, bf16[256,1152]{1,0:T(8,128)(2,1)}, u32[]{:S(2)}) copy-start(bf16[256,1152]{1,0:T(8,128)(2,1)} %param.4) | copy-start | bytes 1769476
  3.2 323.8 %collective-permute-start.2 = (bf16[256,1152]{1,0:T(8,128)(2,1)S(1)}, bf16[256,1152]{1,0:T(8,128)(2,1)S(1)}, u32[]{:S(2)}, u32[]{:S(2)}) collective-permute-start(bf16[256,1152]{1,0:T(8,128)(2,1)S(1)} %fusion.8), channel_id=1, source_target_pairs={{16,0},{32,16},{48,32},{64,48},{80,64},{96,80},{112,96},{128,112},... | collective-permute-start | bytes 1769480 | tf_op jit(solution)/shard_map/ppermute | solution.py:12
  21.7 118.4 %collective-permute-start = (bf16[256,1152]{1,0:T(8,128)(2,1)S(1)}, bf16[256,1152]{1,0:T(8,128)(2,1)S(1)}, u32[]{:S(2)}, u32[]{:S(2)}) collective-permute-start(bf16[256,1152]{1,0:T(8,128)(2,1)S(1)} %fusion.8), channel_id=1, source_target_pairs={{1008,0},{0,16},{16,32},{32,48},{48,64},{64,80},{80,96},{96,112},{... | collective-permute-start | bytes 1769480 | tf_op jit(solution)/shard_map/ppermute | solution.py:12
  141.1 686.3 %collective-permute-start.5 = (f32[256,1152]{1,0:T(8,128)S(1)}, f32[256,1152]{1,0:T(8,128)S(1)}, u32[]{:S(2)}, u32[]{:S(2)}) collective-permute-start(f32[256,1152]{1,0:T(8,128)S(1)} %convolution_multiply_fusion.2), channel_id=1, source_target_pairs={{16,0},{32,16},{48,32},{64,48},{80,64},{96,80},{112,96},{128,112},... | collective-permute-start | bytes 3538952 | tf_op jit(solution)/shard_map/ppermute | solution.py:12
  146.8 292.4 %collective-permute-start.1 = (bf16[256,1152]{1,0:T(8,128)(2,1)S(1)}, bf16[256,1152]{1,0:T(8,128)(2,1)S(1)}, u32[]{:S(2)}, u32[]{:S(2)}) collective-permute-start(bf16[256,1152]{1,0:T(8,128)(2,1)S(1)} %collective-permute-done), channel_id=1, source_target_pairs={{1008,0},{0,16},{16,32},{32,48},{48,64},{64,80},{80,96},{96,112},{... | collective-permute-start | bytes 1769480 | tf_op jit(solution)/shard_map/ppermute | solution.py:12
  328.0 499.4 %collective-permute-start.4 = (f32[256,1152]{1,0:T(8,128)S(1)}, f32[256,1152]{1,0:T(8,128)S(1)}, u32[]{:S(2)}, u32[]{:S(2)}) collective-permute-start(f32[256,1152]{1,0:T(8,128)S(1)} %convolution_multiply_fusion.3), channel_id=1, source_target_pairs={{1008,0},{0,16},{16,32},{32,48},{48,64},{64,80},{80,96},{96,112},{... | collective-permute-start | bytes 3538952 | tf_op jit(solution)/shard_map/ppermute | solution.py:12
  329.9 491.4 %collective-permute-start.3 = (bf16[256,1152]{1,0:T(8,128)(2,1)S(1)}, bf16[256,1152]{1,0:T(8,128)(2,1)S(1)}, u32[]{:S(2)}, u32[]{:S(2)}) collective-permute-start(bf16[256,1152]{1,0:T(8,128)(2,1)S(1)} %collective-permute-done.2), channel_id=1, source_target_pairs={{16,0},{32,16},{48,32},{64,48},{80,64},{96,80},{112,96},{128,112},... | collective-permute-start | bytes 1769480 | tf_op jit(solution)/shard_map/ppermute | solution.py:12
  440.2 387.2 %collective-permute-start.7 = (f32[256,1152]{1,0:T(8,128)S(1)}, f32[256,1152]{1,0:T(8,128)S(1)}, u32[]{:S(2)}, u32[]{:S(2)}) collective-permute-start(f32[256,1152]{1,0:T(8,128)S(1)} %convolution_multiply_fusion), channel_id=1, source_target_pairs={{32,0},{48,16},{64,32},{80,48},{96,64},{112,80},{128,96},{144,112}... | collective-permute-start | bytes 3538952 | tf_op jit(solution)/shard_map/ppermute | solution.py:12
  822.4 196.3 %collective-permute-start.6 = (f32[256,1152]{1,0:T(8,128)S(1)}, f32[256,1152]{1,0:T(8,128)S(1)}, u32[]{:S(2)}, u32[]{:S(2)}) collective-permute-start(f32[256,1152]{1,0:T(8,128)S(1)} %convolution_multiply_fusion.1), channel_id=1, source_target_pairs={{992,0},{1008,16},{0,32},{16,48},{32,64},{48,80},{64,96},{80,112},... | collective-permute-start | bytes 3538952 | tf_op jit(solution)/shard_map/ppermute | solution.py:12
  826.2 192.5 %copy-start.1 = (bf16[256,1152]{1,0:T(8,128)(2,1)S(1)}, bf16[256,1152]{1,0:T(8,128)(2,1)}, u32[]{:S(2)}) copy-start(bf16[256,1152]{1,0:T(8,128)(2,1)} %param.5) | copy-start | bytes 1769476
where the time goes:
time: 1020 us
  waiting for transfers between devices  947 us (93%)
  starting transfers between devices  58.2 us (6%)
    ppermute x8, waiting for transfers between devices, from_behind(): return lax.ppermute(block, axis, route)  947 us
    ppermute x8, starting transfers between devices, from_behind(): return lax.ppermute(block, axis, route)  58.2 us
  transfers between devices with their start and end apart: 8, of which 5 were waited for; matrix products, arithmetic and copies ran while one was open for 1% of the time, Pallas kernels for 0%

commit v1 on v0

v1 whole, which is shorter than its diff:
```python
import jax
import jax.numpy as jnp
from jax import lax
from jax.sharding import PartitionSpec as P

CHUNKS = 2


def move(block, target):
    size = lax.axis_size("blk")
    return lax.ppermute(block, "blk", [(b, target(b) % size) for b in range(size)])


def image_partner(b):
    return b ^ 1


def text_partner(b):
    return b - 1 if b % 2 == 0 else b + 1


def text_relay(b):
    return b - 4 if b % 2 == 0 else b + 4


def image_relay(b):
    return b + 4 if b % 2 == 0 else b - 4


def normalize(embed):
    wide = embed.astype(jnp.float32)
    inv = 1.0 / jnp.sqrt(jnp.sum(wide * wide, axis=-1, keepdims=True) + 1e-06)
    unit = wide * inv
    return (inv, unit, unit.astype(jnp.bfloat16))


def project(inv, unit, grad):
    return inv * (grad - unit * jnp.sum(unit * grad, axis=-1, keepdims=True))


def dot(a, b):
    return jnp.dot(a, b, preferred_element_type=jnp.float32)


def on_device(image_embed, text_embed, log_temp, logit_bias):
    rows = image_embed.shape[0]
    cut = rows // CHUNKS
    scale = jnp.exp(log_temp[0])
    bias = logit_bias[0]

    img_parts, txt_parts = [], []
    for k in range(CHUNKS):
        img_parts.append(move(image_embed[k * cut : (k + 1) * cut], image_partner))
        txt_parts.append(move(text_embed[k * cut : (k + 1) * cut], text_partner))

    def logits_of(img, txt):
        return scale * dot(img, txt.T) + bias

    def summed(logits):
        return jnp.sum(jax.nn.softplus(logits), axis=-1)

    def weigh(logits):
        return jax.nn.sigmoid(logits).astype(jnp.bfloat16)

    inv_i0, unit_i0, i0 = normalize(image_embed)
    inv_t0, unit_t0, t0 = normalize(text_embed)
    eye = jnp.eye(rows, dtype=jnp.float32)
    logits = logits_of(i0, t0)
    loss0 = jnp.sum(jax.nn.softplus((1.0 - 2.0 * eye) * logits), axis=-1)
    w00 = (jax.nn.sigmoid(logits) - eye).astype(jnp.bfloat16)

    img_norm = [normalize(p) for p in img_parts]
    txt_norm = [normalize(p) for p in txt_parts]
    ti_parts = [move(n[2], text_relay) for n in txt_norm]
    ii_parts = [move(n[2], image_relay) for n in img_norm]
    inv_i1, unit_i1, i1 = (jnp.concatenate(v) for v in zip(*img_norm))
    inv_t1, unit_t1, t1 = (jnp.concatenate(v) for v in zip(*txt_norm))

    l01 = logits_of(i0, t1)
    l10 = logits_of(i1, t0)
    l11 = logits_of(i1, t1)
    w01, w10, w11 = weigh(l01), weigh(l10), weigh(l11)
    loss0 = loss0 + summed(l01)
    loss1 = summed(l10) + summed(l11)
    di1 = dot(w10, t0) + dot(w11, t1)
    dt1 = dot(w01.T, i0) + dot(w11.T, i1)

    tr = jnp.concatenate(ti_parts)
    ir = jnp.concatenate(ii_parts)
    l1r = logits_of(i1, tr)
    lr1 = logits_of(ir, t1)
    loss1 = loss1 + summed(l1r)
    di1 = di1 + dot(weigh(l1r), tr)
    dt1 = dt1 + dot(weigh(lr1).T, ir)

    gi1 = project(inv_i1, unit_i1, scale * di1).astype(jnp.bfloat16)
    gt1 = project(inv_t1, unit_t1, scale * dt1).astype(jnp.bfloat16)
    gi = move(gi1, image_partner)
    gt = move(gt1, text_partner)
    loss_in = move(loss1, image_partner)

    di0 = dot(w00, t0) + dot(w01, t1)
    dt0 = dot(w00.T, i0) + dot(w10.T, i1)
    gi0 = project(inv_i0, unit_i0, scale * di0)
    gt0 = project(inv_t0, unit_t0, scale * dt0)
    grad_image = (gi0 + gi.astype(jnp.float32)).astype(jnp.bfloat16)
    grad_text = (gt0 + gt.astype(jnp.float32)).astype(jnp.bfloat16)
    return (loss0 + loss_in, grad_image, grad_text)


def solution(mesh):
    in_specs = (P(("blk", "grp"), None), P(("blk", "grp"), None), P(), P())
    out_specs = (P(("blk", "grp")), P(("blk", "grp"), None), P(("blk", "grp"), None))
    return jax.shard_map(
        on_device, mesh=mesh, in_specs=in_specs, out_specs=out_specs, check_vma=False
    )
```

time: 1020 us -> 299 us (0.29)
  the two profiles are of different devices: /device:TPU:200 before, /device:TPU:2 now
where the time goes in v1:
time: 299 us; the launch traced here: 298 us
  waiting for transfers between devices  187 us (63%)
  starting transfers between devices  74.5 us (25%)
  matrix products  21.9 us (7%)
  other arithmetic  8.36 us (3%)
  local copies, waits for them, and re-layouts  4.28 us (1%)
    ppermute x11, waiting for transfers between devices, move(): lax.ppermute(block, 'blk', [(b, target(b) % size) for b in range(size)])  187 us
    ppermute x11, starting transfers between devices, move(): lax.ppermute(block, 'blk', [(b, target(b) % size) for b in range(size)])  74.5 us
    dot_general x15, matrix products, dot(): return jnp.dot(a, b, preferred_element_type=jnp.float32)  21.9 us
  transfers between devices with their start and end apart: 11, of which 5 were waited for; matrix products, arithmetic and copies ran while one was open for 10% of the time, Pallas kernels for 0%

profile of v1, /device:TPU:2, one launch (start us, length us, event | category | flops | bytes accessed | tf_op | source)
XLA Modules:
  0.0 298.4 jit_solution(2473572182024804706)
XLA Ops:
  0.6 1.2 fusion.69
  1.8 23.1 %collective-permute-start.1 = (bf16[128,1152]{1,0:T(8,128)(2,1)S(1)}, bf16[128,1152]{1,0:T(8,128)(2,1)S(1)}, u32[]{:S(2)}, u32[]{:S(2)}) collective-permute-start(bf16[128,1152]{1,0:T(8,128)(2,1)S(1)} %get-tuple-element.5), channel_id=1, source_target_pairs={{0,1008},{16,32},{32,16},{48,64},{64,48},{80,96},{96,80},{112,128}... | collective-permute-start | bytes 884744 | tf_op jit(solution)/shard_map/ppermute | solution.py:11
  25.0 8.5 %collective-permute-start.2 = (bf16[128,1152]{1,0:T(8,128)(2,1)S(1)}, bf16[128,1152]{1,0:T(8,128)(2,1)S(1)}, u32[]{:S(2)}, u32[]{:S(2)}) collective-permute-start(bf16[128,1152]{1,0:T(8,128)(2,1)S(1)} %get-tuple-element.3), channel_id=1, source_target_pairs={{0,16},{16,0},{32,48},{48,32},{64,80},{80,64},{96,112},{112,96},{1... | collective-permute-start | bytes 884744 | tf_op jit(solution)/shard_map/ppermute | solution.py:11
  33.5 6.1 %collective-permute-start.3 = (bf16[128,1152]{1,0:T(8,128)(2,1)S(1)}, bf16[128,1152]{1,0:T(8,128)(2,1)S(1)}, u32[]{:S(2)}, u32[]{:S(2)}) collective-permute-start(bf16[128,1152]{1,0:T(8,128)(2,1)S(1)} %get-tuple-element.4), channel_id=1, source_target_pairs={{0,16},{16,0},{32,48},{48,32},{64,80},{80,64},{96,112},{112,96},{1... | collective-permute-start | bytes 884744 | tf_op jit(solution)/shard_map/ppermute | solution.py:11
  39.6 1.9 collective-permute-start
  41.5 0.2 fusion.15
  41.7 0.2 fusion.21
  43.3 1.1 fusion.37
  44.4 0.4 fusion.58
  44.8 0.4 fusion.59
  45.2 73.6 %collective-permute-done.1 = bf16[128,1152]{1,0:T(8,128)(2,1)S(1)} collective-permute-done((bf16[128,1152]{1,0:T(8,128)(2,1)S(1)}, bf16[128,1152]{1,0:T(8,128)(2,1)S(1)}, u32[]{:S(2)}, u32[]{:S(2)}) %collective-permute-start.1) | collective-permute-done | bytes 294944 | tf_op jit(solution)/shard_map/ppermute | solution.py:11
  118.9 0.1 fusion.34
  119.0 7.3 %collective-permute-done.2 = bf16[128,1152]{1,0:T(8,128)(2,1)S(1)} collective-permute-done((bf16[128,1152]{1,0:T(8,128)(2,1)S(1)}, bf16[128,1152]{1,0:T(8,128)(2,1)S(1)}, u32[]{:S(2)}, u32[]{:S(2)}) %collective-permute-start.2) | collective-permute-done | bytes 294944 | tf_op jit(solution)/shard_map/ppermute | solution.py:11
  126.3 0.1 fusion.35
  126.4 12.6 %collective-permute-done.3 = bf16[128,1152]{1,0:T(8,128)(2,1)S(1)} collective-permute-done((bf16[128,1152]{1,0:T(8,128)(2,1)S(1)}, bf16[128,1152]{1,0:T(8,128)(2,1)S(1)}, u32[]{:S(2)}, u32[]{:S(2)}) %collective-permute-start.3) | collective-permute-done | bytes 294944 | tf_op jit(solution)/shard_map/ppermute | solution.py:11
  139.0 0.1 fusion.36
  139.2 0.1 fusion.33
  139.5 3.4 %collective-permute-start.8 = (bf16[128,1152]{1,0:T(8,128)(2,1)S(1)}, bf16[128,1152]{1,0:T(8,128)(2,1)S(1)}, u32[]{:S(2)}, u32[]{:S(2)}) collective-permute-start(bf16[128,1152]{1,0:T(8,128)(2,1)S(1)} %get-tuple-element.12), channel_id=1, source_target_pairs={{0,64},{16,976},{32,96},{48,1008},{64,128},{80,16},{96,160},{112,4... | collective-permute-start | bytes 884744 | tf_op jit(solution)/shard_map/ppermute | solution.py:11
  143.0 3.4 %collective-permute-start.9 = (bf16[128,1152]{1,0:T(8,128)(2,1)S(1)}, bf16[128,1152]{1,0:T(8,128)(2,1)S(1)}, u32[]{:S(2)}, u32[]{:S(2)}) collective-permute-start(bf16[128,1152]{1,0:T(8,128)(2,1)S(1)} %get-tuple-element.14), channel_id=1, source_target_pairs={{0,64},{16,976},{32,96},{48,1008},{64,128},{80,16},{96,160},{112,4... | collective-permute-start | bytes 884744 | tf_op jit(solution)/shard_map/ppermute | solution.py:11
  146.4 1.0 convert_multiply_fusion.8
  147.5 4.1 %collective-permute-start.5 = (bf16[128,1152]{1,0:T(8,128)(2,1)}, bf16[128,1152]{1,0:T(8,128)(2,1)}, u32[]{:S(2)}, u32[]{:S(2)}) collective-permute-start(bf16[128,1152]{1,0:T(8,128)(2,1)} %get-tuple-element.10), channel_id=1, source_target_pairs={{0,960},{16,80},{32,992},{48,112},{64,0},{80,144},{96,32},{112,176... | collective-permute-start | bytes 884744 | tf_op jit(solution)/shard_map/ppermute | solution.py:11
  151.6 1.0 convert_multiply_fusion.10
  152.6 7.2 %collective-permute-start.4 = (bf16[128,1152]{1,0:T(8,128)(2,1)}, bf16[128,1152]{1,0:T(8,128)(2,1)}, u32[]{:S(2)}, u32[]{:S(2)}) collective-permute-start(bf16[128,1152]{1,0:T(8,128)(2,1)} %get-tuple-element.8), channel_id=1, source_target_pairs={{0,960},{16,80},{32,992},{48,112},{64,0},{80,144},{96,32},{112,176... | collective-permute-start | bytes 884744 | tf_op jit(solution)/shard_map/ppermute | solution.py:11
  159.9 2.1 fusion.40
  162.0 2.2 fusion.38
  164.2 0.4 fusion.56
  164.6 1.1 fusion.39
  165.7 0.4 fusion.57
  166.1 2.1 fusion.16
  168.2 3.1 %fusion.10 = (f32[256]{0:T(256)}, f32[256,1152]{1,0:T(8,128)}) fusion(bf16[256,1152]{1,0:T(8,128)(2,1)S(1)} %copy-done.1, f32[256]{0:T(256)S(1)} %add_rsqrt_fusion.1, f32[256,1152]{1,0:T(8,128)S(1)} %fusion.59, bf16[128,1152]{1,0:T(8,128)(2,1)} %get-tuple-element.10, bf16[128,1152]{1,0:T(8,128)(2,1)} %get-tuple-element.8, ...), kind=kOutput, calls=%fused_computation.20 | convolution fusion | flops 154205952 | bytes 3803140 | tf_op jit(solution)/shard_map/dot_general | solution.py:42
  171.2 1.4 convolution_add_fusion.1
  172.6 1.5 convolution_add_fusion.4
  174.2 0.8 copy-done.8
  175.1 4.7 %multiply_reduce_fusion = (f32[256]{0:T(256)}, f32[256,1152]{1,0:T(8,128)}) fusion(f32[128,1152]{1,0:T(8,128)} %get-tuple-element.9, f32[128,1152]{1,0:T(8,128)} %get-tuple-element.7, f32[256,1152]{1,0:T(8,128)} %convolution_add_fusion.1, bf16[256,1152]{1,0:T(8,128)(2,1)} %copy-done.8, f32[]{:T(128)} %bitcast.17, f32[]{:T(128)} %bitcast, ...), kind=kOutput, calls=%fused_computation.35 | convolution fusion | flops 305037056 | bytes 4719624 | tf_op jit(solution)/shard_map/dot_general | solution.py:42
  179.8 1.8 multiply_convert_fusion
  181.6 2.1 collective-permute-start.10
  183.7 1.0 constant_dynamic-update-slice_fusion.1
  184.7 1.0 constant_dynamic-update-slice_fusion
  185.7 0.5 fusion.41
  186.4 4.1 %collective-permute-start.6 = (f32[256]{0:T(256)S(1)}, f32[256]{0:T(256)S(1)}, u32[]{:S(2)}, u32[]{:S(2)}) collective-permute-start(f32[256]{0:T(256)S(1)} %add_add_fusion), channel_id=1, source_target_pairs={{0,16},{16,0},{32,48},{48,32},{64,80},{80,64},{96,112},{112,96},{1... | collective-permute-start | bytes 3080 | tf_op jit(solution)/shard_map/ppermute | solution.py:11
  190.5 0.5 multiply_reduce_fusion.1
  191.1 0.3 multiply_convert_fusion.1
  191.3 10.6 %collective-permute-start.7 = (bf16[256,1152]{1,0:T(8,128)(2,1)S(1)}, bf16[256,1152]{1,0:T(8,128)(2,1)S(1)}, u32[]{:S(2)}, u32[]{:S(2)}) collective-permute-start(bf16[256,1152]{1,0:T(8,128)(2,1)S(1)} %multiply_convert_fusion.1), channel_id=1, source_target_pairs={{0,16},{16,0},{32,48},{48,32},{64,80},{80,64},{96,112},{112,96},{1... | collective-permute-start | bytes 1769480 | tf_op jit(solution)/shard_map/ppermute | solution.py:11
  201.9 0.6 add_add_fusion.1
  202.5 84.8 %collective-permute-done.10 = bf16[256,1152]{1,0:T(8,128)(2,1)S(1)} collective-permute-done((bf16[256,1152]{1,0:T(8,128)(2,1)S(1)}, bf16[256,1152]{1,0:T(8,128)(2,1)S(1)}, u32[]{:S(2)}, u32[]{:S(2)}) %collective-permute-start.10) | collective-permute-done | bytes 589856 | tf_op jit(solution)/shard_map/ppermute | solution.py:11
  287.3 1.2 fusion.20
  288.4 8.7 %collective-permute-done.7 = bf16[256,1152]{1,0:T(8,128)(2,1)S(1)} collective-permute-done((bf16[256,1152]{1,0:T(8,128)(2,1)S(1)}, bf16[256,1152]{1,0:T(8,128)(2,1)S(1)}, u32[]{:S(2)}, u32[]{:S(2)}) %collective-permute-start.7) | collective-permute-done | bytes 589856 | tf_op jit(solution)/shard_map/ppermute | solution.py:11
  297.2 1.2 fusion.14
  (49 shorter events, 0.7 us)
Async XLA Ops:
  0.6 24.3 %copy-start.1 = (bf16[256,1152]{1,0:T(8,128)(2,1)S(1)}, bf16[256,1152]{1,0:T(8,128)(2,1)}, u32[]{:S(2)}) copy-start(bf16[256,1152]{1,0:T(8,128)(2,1)} %param.4) | copy-start | bytes 1769476
  1.8 39.9 %copy-start = (bf16[256,1152]{1,0:T(8,128)(2,1)S(1)}, bf16[256,1152]{1,0:T(8,128)(2,1)}, u32[]{:S(2)}) copy-start(bf16[256,1152]{1,0:T(8,128)(2,1)} %param.5) | copy-start | bytes 1769476
  1.8 117.0 %collective-permute-start.1 = (bf16[128,1152]{1,0:T(8,128)(2,1)S(1)}, bf16[128,1152]{1,0:T(8,128)(2,1)S(1)}, u32[]{:S(2)}, u32[]{:S(2)}) collective-permute-start(bf16[128,1152]{1,0:T(8,128)(2,1)S(1)} %get-tuple-element.5), channel_id=1, source_target_pairs={{0,1008},{16,32},{32,16},{48,64},{64,48},{80,96},{96,80},{112,128}... | collective-permute-start | bytes 884744 | tf_op jit(solution)/shard_map/ppermute | solution.py:11
  25.0 101.3 %collective-permute-start.2 = (bf16[128,1152]{1,0:T(8,128)(2,1)S(1)}, bf16[128,1152]{1,0:T(8,128)(2,1)S(1)}, u32[]{:S(2)}, u32[]{:S(2)}) collective-permute-start(bf16[128,1152]{1,0:T(8,128)(2,1)S(1)} %get-tuple-element.3), channel_id=1, source_target_pairs={{0,16},{16,0},{32,48},{48,32},{64,80},{80,64},{96,112},{112,96},{1... | collective-permute-start | bytes 884744 | tf_op jit(solution)/shard_map/ppermute | solution.py:11
  33.5 105.5 %collective-permute-start.3 = (bf16[128,1152]{1,0:T(8,128)(2,1)S(1)}, bf16[128,1152]{1,0:T(8,128)(2,1)S(1)}, u32[]{:S(2)}, u32[]{:S(2)}) collective-permute-start(bf16[128,1152]{1,0:T(8,128)(2,1)S(1)} %get-tuple-element.4), channel_id=1, source_target_pairs={{0,16},{16,0},{32,48},{48,32},{64,80},{80,64},{96,112},{112,96},{1... | collective-permute-start | bytes 884744 | tf_op jit(solution)/shard_map/ppermute | solution.py:11
  39.6 99.6 %collective-permute-start = (bf16[128,1152]{1,0:T(8,128)(2,1)S(1)}, bf16[128,1152]{1,0:T(8,128)(2,1)S(1)}, u32[]{:S(2)}, u32[]{:S(2)}) collective-permute-start(bf16[128,1152]{1,0:T(8,128)(2,1)S(1)} %get-tuple-element.6), channel_id=1, source_target_pairs={{0,1008},{16,32},{32,16},{48,64},{64,48},{80,96},{96,80},{112,128}... | collective-permute-start | bytes 884744 | tf_op jit(solution)/shard_map/ppermute | solution.py:11
  139.5 31.8 %copy-start.2 = (bf16[128,1152]{1,0:T(8,128)(2,1)}, bf16[128,1152]{1,0:T(8,128)(2,1)S(1)}, u32[]{:S(2)}) copy-start(bf16[128,1152]{1,0:T(8,128)(2,1)S(1)} %get-tuple-element.12) | copy-start | bytes 884740
  139.5 34.7 %collective-permute-start.8 = (bf16[128,1152]{1,0:T(8,128)(2,1)S(1)}, bf16[128,1152]{1,0:T(8,128)(2,1)S(1)}, u32[]{:S(2)}, u32[]{:S(2)}) collective-permute-start(bf16[128,1152]{1,0:T(8,128)(2,1)S(1)} %get-tuple-element.12), channel_id=1, source_target_pairs={{0,64},{16,976},{32,96},{48,1008},{64,128},{80,16},{96,160},{112,4... | collective-permute-start | bytes 884744 | tf_op jit(solution)/shard_map/ppermute | solution.py:11
  143.0 28.2 %copy-start.4 = (bf16[128,1152]{1,0:T(8,128)(2,1)}, bf16[128,1152]{1,0:T(8,128)(2,1)S(1)}, u32[]{:S(2)}) copy-start(bf16[128,1152]{1,0:T(8,128)(2,1)S(1)} %get-tuple-element.14) | copy-start | bytes 884740
  143.0 31.2 %collective-permute-start.9 = (bf16[128,1152]{1,0:T(8,128)(2,1)S(1)}, bf16[128,1152]{1,0:T(8,128)(2,1)S(1)}, u32[]{:S(2)}, u32[]{:S(2)}) collective-permute-start(bf16[128,1152]{1,0:T(8,128)(2,1)S(1)} %get-tuple-element.14), channel_id=1, source_target_pairs={{0,64},{16,976},{32,96},{48,1008},{64,128},{80,16},{96,160},{112,4... | collective-permute-start | bytes 884744 | tf_op jit(solution)/shard_map/ppermute | solution.py:11
  147.5 37.2 %collective-permute-start.5 = (bf16[128,1152]{1,0:T(8,128)(2,1)}, bf16[128,1152]{1,0:T(8,128)(2,1)}, u32[]{:S(2)}, u32[]{:S(2)}) collective-permute-start(bf16[128,1152]{1,0:T(8,128)(2,1)} %get-tuple-element.10), channel_id=1, source_target_pairs={{0,960},{16,80},{32,992},{48,112},{64,0},{80,144},{96,32},{112,176... | collective-permute-start | bytes 884744 | tf_op jit(solution)/shard_map/ppermute | solution.py:11
  152.6 31.0 %collective-permute-start.4 = (bf16[128,1152]{1,0:T(8,128)(2,1)}, bf16[128,1152]{1,0:T(8,128)(2,1)}, u32[]{:S(2)}, u32[]{:S(2)}) collective-permute-start(bf16[128,1152]{1,0:T(8,128)(2,1)} %get-tuple-element.8), channel_id=1, source_target_pairs={{0,960},{16,80},{32,992},{48,112},{64,0},{80,144},{96,32},{112,176... | collective-permute-start | bytes 884744 | tf_op jit(solution)/shard_map/ppermute | solution.py:11
  174.2 0.8 copy-start.8
  181.6 4.1 %copy-start.3 = (bf16[128,1152]{1,0:T(8,128)(2,1)S(1)}, bf16[128,1152]{1,0:T(8,128)(2,1)}, u32[]{:S(2)}) copy-start(bf16[128,1152]{1,0:T(8,128)(2,1)} %copy-done.2) | copy-start | bytes 884740
  181.6 4.1 %copy-start.5 = (bf16[128,1152]{1,0:T(8,128)(2,1)S(1)}, bf16[128,1152]{1,0:T(8,128)(2,1)}, u32[]{:S(2)}) copy-start(bf16[128,1152]{1,0:T(8,128)(2,1)} %copy-done.4) | copy-start | bytes 884740
  181.6 105.6 %collective-permute-start.10 = (bf16[256,1152]{1,0:T(8,128)(2,1)S(1)}, bf16[256,1152]{1,0:T(8,128)(2,1)S(1)}, u32[]{:S(2)}, u32[]{:S(2)}) collective-permute-start(bf16[256,1152]{1,0:T(8,128)(2,1)S(1)} %multiply_convert_fusion), channel_id=1, source_target_pairs={{0,1008},{16,32},{32,16},{48,64},{64,48},{80,96},{96,80},{112,128}... | collective-permute-start | bytes 1769480 | tf_op jit(solution)/shard_map/ppermute | solution.py:11
  185.7 0.7 copy-start.13
  185.7 0.7 copy-start.14
  186.4 15.5 %collective-permute-start.6 = (f32[256]{0:T(256)S(1)}, f32[256]{0:T(256)S(1)}, u32[]{:S(2)}, u32[]{:S(2)}) collective-permute-start(f32[256]{0:T(256)S(1)} %add_add_fusion), channel_id=1, source_target_pairs={{0,16},{16,0},{32,48},{48,32},{64,80},{80,64},{96,112},{112,96},{1... | collective-permute-start | bytes 3080 | tf_op jit(solution)/shard_map/ppermute | solution.py:11
  191.0 10.9 %copy-start.11 = (f32[256]{0:T(256)S(1)}, f32[256]{0:T(256)}, u32[]{:S(2)}) copy-start(f32[256]{0:T(256)} %get-tuple-element.29) | copy-start | bytes 3076
  191.0 10.9 %copy-start.12 = (f32[256]{0:T(256)S(1)}, f32[256]{0:T(256)}, u32[]{:S(2)}) copy-start(f32[256]{0:T(256)} %get-tuple-element.31) | copy-start | bytes 3076
  191.0 96.2 %copy-start.7 = (f32[256,1152]{1,0:T(8,128)S(1)}, f32[256,1152]{1,0:T(8,128)}, u32[]{:S(2)}) copy-start(f32[256,1152]{1,0:T(8,128)} %get-tuple-element.40) | copy-start | bytes 3538948
  191.0 96.2 %copy-start.10 = (f32[256]{0:T(256)S(1)}, f32[256]{0:T(256)}, u32[]{:S(2)}) copy-start(f32[256]{0:T(256)} %get-tuple-element.39) | copy-start | bytes 3076
  191.3 105.9 %collective-permute-start.7 = (bf16[256,1152]{1,0:T(8,128)(2,1)S(1)}, bf16[256,1152]{1,0:T(8,128)(2,1)S(1)}, u32[]{:S(2)}, u32[]{:S(2)}) collective-permute-start(bf16[256,1152]{1,0:T(8,128)(2,1)S(1)} %multiply_convert_fusion.1), channel_id=1, source_target_pairs={{0,16},{16,0},{32,48},{48,32},{64,80},{80,64},{96,112},{112,96},{1... | collective-permute-start | bytes 1769480 | tf_op jit(solution)/shard_map/ppermute | solution.py:11
  287.3 9.9 %copy-start.6 = (f32[256,1152]{1,0:T(8,128)S(1)}, f32[256,1152]{1,0:T(8,128)}, u32[]{:S(2)}) copy-start(f32[256,1152]{1,0:T(8,128)} %get-tuple-element.36) | copy-start | bytes 3538948
  287.3 9.9 %copy-start.9 = (f32[256]{0:T(256)S(1)}, f32[256]{0:T(256)}, u32[]{:S(2)}) copy-start(f32[256]{0:T(256)} %get-tuple-element.35) | copy-start | bytes 3076

commit v2 on v0

v2 whole, which is shorter than its diff:
```python
import jax
import jax.numpy as jnp
from jax import lax
from jax.experimental import pallas as pl
from jax.experimental.pallas import tpu as pltpu
from jax.sharding import PartitionSpec as P

def paired(b, n):
    return b ^ 1


def crossed(b, n):
    return (b - 1 if b % 2 == 0 else b + 1) % n


def ring_out(b, n):
    return (b - 4 if b % 2 == 0 else b + 4) % n


def ring_back(b, n):
    return (b + 4 if b % 2 == 0 else b - 4) % n


def move(block, even, odd):
    n_blk, n_grp = lax.axis_size("blk"), lax.axis_size("grp")
    route = [
        (b * n_grp + g, (odd if g % 2 else even)(b, n_blk) * n_grp + g)
        for b in range(n_blk)
        for g in range(n_grp)
    ]
    return lax.ppermute(block, ("blk", "grp"), route)


def swap_image(block):
    return move(block, paired, crossed)


def swap_text(block):
    return move(block, crossed, paired)


def pass_text(block):
    return move(block, ring_out, ring_back)


def pass_image(block):
    return move(block, ring_back, ring_out)


def normalize(ref):
    wide = ref[...].astype(jnp.float32)
    inv = lax.rsqrt(jnp.sum(wide * wide, axis=-1, keepdims=True) + 1e-06)
    unit = wide * inv
    return inv, unit, unit.astype(jnp.bfloat16)


def project(inv, unit, grad):
    return inv * (grad - unit * jnp.sum(unit * grad, axis=-1, keepdims=True))


def dot_nt(a, b):
    return lax.dot_general(a, b, (((1,), (1,)), ((), ())), preferred_element_type=jnp.float32)


def dot_nn(a, b):
    return jnp.dot(a, b, preferred_element_type=jnp.float32)


def dot_tn(a, b):
    return lax.dot_general(a, b, (((0,), (0,)), ((), ())), preferred_element_type=jnp.float32)


def pair_of(scalars, img, txt, own=False):
    logits = scalars[0] * dot_nt(img, txt) + scalars[1]
    small = jnp.exp(-jnp.abs(logits))
    part = 1.0 / (1.0 + small)
    weights = jnp.where(logits >= 0, part, small * part)
    if own:
        hit = lax.broadcasted_iota(jnp.int32, logits.shape, 0) == lax.broadcasted_iota(
            jnp.int32, logits.shape, 1
        )
        weights = jnp.where(hit, weights - 1.0, weights)
        logits = jnp.where(hit, -logits, logits)
    losses = jnp.sum(jnp.maximum(logits, 0.0) + jnp.log1p(small), axis=-1, keepdims=True)
    return losses, weights.astype(jnp.bfloat16)


def main_kernel(scalars, i0_ref, t0_ref, i1_ref, t1_ref, gi0, gt0, di1, dt1, loss0, loss1):
    scale = scalars[0]
    inv_i0, unit_i0, i0 = normalize(i0_ref)
    inv_t0, unit_t0, t0 = normalize(t0_ref)
    _, _, i1 = normalize(i1_ref)
    _, _, t1 = normalize(t1_ref)
    a, w00 = pair_of(scalars, i0, t0, own=True)
    b, w01 = pair_of(scalars, i0, t1)
    loss0[...] = a + b
    a, w10 = pair_of(scalars, i1, t0)
    b, w11 = pair_of(scalars, i1, t1)
    loss1[...] = a + b
    di1[...] = dot_nn(w10, t0) + dot_nn(w11, t1)
    dt1[...] = dot_tn(w01, i0) + dot_tn(w11, i1)
    gi0[...] = project(inv_i0, unit_i0, scale * (dot_nn(w00, t0) + dot_nn(w01, t1)))
    gt0[...] = project(inv_t0, unit_t0, scale * (dot_tn(w00, i0) + dot_tn(w10, i1)))


def rest_kernel(scalars, i1_ref, t1_ref, ir_ref, tr_ref, di1, dt1, loss1, gi1, gt1, loss):
    scale = scalars[0]
    inv_i1, unit_i1, i1 = normalize(i1_ref)
    inv_t1, unit_t1, t1 = normalize(t1_ref)
    _, _, ir = normalize(ir_ref)
    _, _, tr = normalize(tr_ref)
    a, w1r = pair_of(scalars, i1, tr)
    loss[...] = loss1[...] + a
    _, wr1 = pair_of(scalars, ir, t1)
    gi1[...] = project(inv_i1, unit_i1, scale * (di1[...] + dot_nn(w1r, tr))).astype(jnp.bfloat16)
    gt1[...] = project(inv_t1, unit_t1, scale * (dt1[...] + dot_tn(wr1, ir))).astype(jnp.bfloat16)


def call(kernel, name, outs, flops, *args):
    vmem = pl.BlockSpec(memory_space=pltpu.VMEM)
    return pl.pallas_call(
        kernel,
        name=name,
        out_shape=outs,
        in_specs=[pl.BlockSpec(memory_space=pltpu.SMEM)] + [vmem] * (len(args) - 1),
        out_specs=[vmem] * len(outs),
        compiler_params=pltpu.CompilerParams(vmem_limit_bytes=40 * 1024 * 1024),
        cost_estimate=pl.CostEstimate(
            flops=flops, bytes_accessed=8 * 1024 * 1024, transcendentals=0
        ),
    )(*args)


def on_device(image_embed, text_embed, log_temp, logit_bias):
    rows, wide = image_embed.shape
    scalars = jnp.concatenate([jnp.exp(log_temp), logit_bias])
    full = jax.ShapeDtypeStruct((rows, wide), jnp.float32)
    half = jax.ShapeDtypeStruct((rows, wide), jnp.bfloat16)
    column = jax.ShapeDtypeStruct((rows, 1), jnp.float32)
    product = 2 * rows * rows * wide

    i1 = swap_image(image_embed)
    t1 = swap_text(text_embed)
    ir = pass_image(i1)
    tr = pass_text(t1)
    gi0, gt0, di1, dt1, loss0, loss1 = call(
        main_kernel, "main", [full] * 4 + [column] * 2, 12 * product,
        scalars, image_embed, text_embed, i1, t1,
    )
    gi1, gt1, loss1 = call(
        rest_kernel, "rest", [half, half, column], 4 * product,
        scalars, i1, t1, ir, tr, di1, dt1, loss1,
    )
    gi = swap_image(gi1)
    gt = swap_text(gt1)
    loss_in = swap_image(loss1.reshape(rows))
    grad_image = (gi0 + gi.astype(jnp.float32)).astype(jnp.bfloat16)
    grad_text = (gt0 + gt.astype(jnp.float32)).astype(jnp.bfloat16)
    return (loss0.reshape(rows) + loss_in, grad_image, grad_text)


def solution(mesh):
    in_specs = (P(("blk", "grp"), None), P(("blk", "grp"), None), P(), P())
    out_specs = (P(("blk", "grp")), P(("blk", "grp"), None), P(("blk", "grp"), None))
    return jax.shard_map(
        on_device, mesh=mesh, in_specs=in_specs, out_specs=out_specs, check_vma=False
    )
```

time: 1020 us -> 256 us (0.25)
  the two profiles are of different devices: /device:TPU:200 before, /device:TPU:113 now
where the time goes in v2:
time: 256 us
  waiting for transfers between devices  168 us (66%)
  starting transfers between devices  72 us (28%)
  Pallas kernels  7.04 us (3%)
  other arithmetic  4.81 us (2%)
    ppermute x7, waiting for transfers between devices, move(): return lax.ppermute(block, ('blk', 'grp'), route)  168 us
    ppermute x7, starting transfers between devices, move(): return lax.ppermute(block, ('blk', 'grp'), route)  72 us
    pallas_call x2, Pallas kernels, call(): pl.pallas_call(kernel, name=name, out_shape=outs, in_specs=[pl.BlockSpec(...  7.04 us
  transfers between devices with their start and end apart: 7, of which 3 were waited for; matrix products, arithmetic and copies ran while one was open for 1% of the time, Pallas kernels for 2%

profile of v2, /device:TPU:113, one launch (start us, length us, event | category | flops | bytes accessed | tf_op | source)
XLA Modules:
  0.0 255.8 jit_solution(13560964877239796335)
XLA Ops:
  0.6 22.1 %collective-permute-start = (bf16[256,1152]{1,0:T(8,128)(2,1)}, bf16[256,1152]{1,0:T(8,128)(2,1)S(1)}, u32[]{:S(2)}, u32[]{:S(2)}) collective-permute-start(bf16[256,1152]{1,0:T(8,128)(2,1)} %i0_ref.1), channel_id=1, source_target_pairs={{0,16},{1,1009},{2,18},{3,1011},{4,20},{5,1013},{6,22},{7,1015},{8... | collective-permute-start | bytes 1769480 | tf_op jit(solution)/shard_map/ppermute | solution.py:31
  22.7 6.1 %collective-permute-start.1 = (bf16[256,1152]{1,0:T(8,128)(2,1)}, bf16[256,1152]{1,0:T(8,128)(2,1)S(1)}, u32[]{:S(2)}, u32[]{:S(2)}) collective-permute-start(bf16[256,1152]{1,0:T(8,128)(2,1)} %t0_ref.1), channel_id=1, source_target_pairs={{0,1008},{1,17},{2,1010},{3,19},{4,1012},{5,21},{6,1014},{7,23},{8... | collective-permute-start | bytes 1769480 | tf_op jit(solution)/shard_map/ppermute | solution.py:31
  28.8 80.1 %collective-permute-done.i1_ref = bf16[256,1152]{1,0:T(8,128)(2,1)S(1)} collective-permute-done((bf16[256,1152]{1,0:T(8,128)(2,1)}, bf16[256,1152]{1,0:T(8,128)(2,1)S(1)}, u32[]{:S(2)}, u32[]{:S(2)}) %collective-permute-start) | collective-permute-done | bytes 589856 | tf_op jit(solution)/shard_map/ppermute | solution.py:31
  108.9 2.4 collective-permute-start.2
  111.4 0.0 collective-permute-done.1.t1_ref
  111.4 2.8 %collective-permute-start.3 = (bf16[256,1152]{1,0:T(8,128)(2,1)S(1)}, bf16[256,1152]{1,0:T(8,128)(2,1)S(1)}, u32[]{:S(2)}, u32[]{:S(2)}) collective-permute-start(bf16[256,1152]{1,0:T(8,128)(2,1)S(1)} %collective-permute-done.1.t1_ref), channel_id=1, source_target_pairs={{0,960},{1,65},{2,962},{3,67},{4,964},{5,69},{6,966},{7,71},{8,968... | collective-permute-start | bytes 1769480 | tf_op jit(solution)/shard_map/ppermute | solution.py:31
  115.6 0.1 pad_maximum_fusion.scalars
  115.6 0.0 copy-start
  115.6 1.1 copy-done
  116.7 0.0 copy-start.1
  116.7 1.1 copy-done.1
  117.8 3.8 %main.1 = (f32[256,1152]{1,0:T(8,128)S(1)}, f32[256,1152]{1,0:T(8,128)S(1)}, f32[256,1152]{1,0:T(8,128)S(1)}, f32[256,1152]{1,0:T(8,128)S(1)}, f32[256,1]{1,0:T(8,128)S(1)}, /*index=5*/f32[256,1]{1,0:T(8,128)S(1)}) custom-call(f32[2]{0:T(128)S(1)} %pad_maximum_fusion.scalars, bf16[256,1152]{1,0:T(8,128)(2,1)S(1)} %copy-done, ...), custom_call_target="tpu_custom_call" | custom-call | flops 1811939328 | bytes 8388608 | tf_op jit(solution)/shard_map/main/pallas_call | solution.py:121
  121.6 0.0 collective-permute-done.2.ir_ref
  121.6 2.5 collective-permute-done.3.tr_ref
  124.2 3.2 %rest.1 = (bf16[256,1152]{1,0:T(8,128)(2,1)}, bf16[256,1152]{1,0:T(8,128)(2,1)S(1)}, f32[256,1]{1,0:T(8,128)S(1)}) custom-call(f32[2]{0:T(128)S(1)} %pad_maximum_fusion.scalars, bf16[256,1152]{1,0:T(8,128)(2,1)S(1)} %collective-permute-done.i1_ref, bf16[256,1152]{1,0:T(8,128)(2,1)S(1)} %collective-permute-done.1.t1_ref, ...), custom_call_target="tpu_custom_call" | custom-call | flops 603979776 | bytes 8388608 | tf_op jit(solution)/shard_map/rest/pallas_call | solution.py:121
  127.4 26.3 %collective-permute-start.5 = (bf16[256,1152]{1,0:T(8,128)(2,1)}, bf16[256,1152]{1,0:T(8,128)(2,1)}, u32[]{:S(2)}, u32[]{:S(2)}) collective-permute-start(bf16[256,1152]{1,0:T(8,128)(2,1)} %get-tuple-element.18), channel_id=1, source_target_pairs={{0,16},{1,1009},{2,18},{3,1011},{4,20},{5,1013},{6,22},{7,1015},{8... | collective-permute-start | bytes 1769480 | tf_op jit(solution)/shard_map/ppermute | solution.py:31
  153.7 10.3 %collective-permute-start.6 = (bf16[256,1152]{1,0:T(8,128)(2,1)S(1)}, bf16[256,1152]{1,0:T(8,128)(2,1)}, u32[]{:S(2)}, u32[]{:S(2)}) collective-permute-start(bf16[256,1152]{1,0:T(8,128)(2,1)S(1)} %get-tuple-element.20), channel_id=1, source_target_pairs={{0,1008},{1,17},{2,1010},{3,19},{4,1012},{5,21},{6,1014},{7,23},{8... | collective-permute-start | bytes 1769480 | tf_op jit(solution)/shard_map/ppermute | solution.py:31
  164.0 0.1 reduce.1
  164.1 1.9 collective-permute-start.4
  166.0 0.1 reduce
  166.1 85.2 %collective-permute-done.4 = f32[256]{0:T(256)S(1)} collective-permute-done((f32[256]{0:T(256)S(1)}, f32[256]{0:T(256)S(1)}, u32[]{:S(2)}, u32[]{:S(2)}) %collective-permute-start.4) | collective-permute-done | bytes 1056 | tf_op jit(solution)/shard_map/ppermute | solution.py:31
  251.3 0.6 add.9
  251.9 0.0 collective-permute-done.5
  251.9 2.0 add_convert_fusion.1
  253.9 0.0 collective-permute-done.6
  253.9 2.0 add_convert_fusion
Async XLA Ops:
  0.6 108.3 %collective-permute-start = (bf16[256,1152]{1,0:T(8,128)(2,1)}, bf16[256,1152]{1,0:T(8,128)(2,1)S(1)}, u32[]{:S(2)}, u32[]{:S(2)}) collective-permute-start(bf16[256,1152]{1,0:T(8,128)(2,1)} %i0_ref.1), channel_id=1, source_target_pairs={{0,16},{1,1009},{2,18},{3,1011},{4,20},{5,1013},{6,22},{7,1015},{8... | collective-permute-start | bytes 1769480 | tf_op jit(solution)/shard_map/ppermute | solution.py:31
  22.7 88.6 %collective-permute-start.1 = (bf16[256,1152]{1,0:T(8,128)(2,1)}, bf16[256,1152]{1,0:T(8,128)(2,1)S(1)}, u32[]{:S(2)}, u32[]{:S(2)}) collective-permute-start(bf16[256,1152]{1,0:T(8,128)(2,1)} %t0_ref.1), channel_id=1, source_target_pairs={{0,1008},{1,17},{2,1010},{3,19},{4,1012},{5,21},{6,1014},{7,23},{8... | collective-permute-start | bytes 1769480 | tf_op jit(solution)/shard_map/ppermute | solution.py:31
  108.9 12.7 %collective-permute-start.2 = (bf16[256,1152]{1,0:T(8,128)(2,1)S(1)}, bf16[256,1152]{1,0:T(8,128)(2,1)S(1)}, u32[]{:S(2)}, u32[]{:S(2)}) collective-permute-start(bf16[256,1152]{1,0:T(8,128)(2,1)S(1)} %collective-permute-done.i1_ref), channel_id=1, source_target_pairs={{0,64},{1,961},{2,66},{3,963},{4,68},{5,965},{6,70},{7,967},{8,72}... | collective-permute-start | bytes 1769480 | tf_op jit(solution)/shard_map/ppermute | solution.py:31
  111.4 12.8 %collective-permute-start.3 = (bf16[256,1152]{1,0:T(8,128)(2,1)S(1)}, bf16[256,1152]{1,0:T(8,128)(2,1)S(1)}, u32[]{:S(2)}, u32[]{:S(2)}) collective-permute-start(bf16[256,1152]{1,0:T(8,128)(2,1)S(1)} %collective-permute-done.1.t1_ref), channel_id=1, source_target_pairs={{0,960},{1,65},{2,962},{3,67},{4,964},{5,69},{6,966},{7,71},{8,968... | collective-permute-start | bytes 1769480 | tf_op jit(solution)/shard_map/ppermute | solution.py:31
  115.6 1.1 copy-start
  116.7 1.1 copy-start.1
  127.4 124.5 %collective-permute-start.5 = (bf16[256,1152]{1,0:T(8,128)(2,1)}, bf16[256,1152]{1,0:T(8,128)(2,1)}, u32[]{:S(2)}, u32[]{:S(2)}) collective-permute-start(bf16[256,1152]{1,0:T(8,128)(2,1)} %get-tuple-element.18), channel_id=1, source_target_pairs={{0,16},{1,1009},{2,18},{3,1011},{4,20},{5,1013},{6,22},{7,1015},{8... | collective-permute-start | bytes 1769480 | tf_op jit(solution)/shard_map/ppermute | solution.py:31
  153.7 100.1 %collective-permute-start.6 = (bf16[256,1152]{1,0:T(8,128)(2,1)S(1)}, bf16[256,1152]{1,0:T(8,128)(2,1)}, u32[]{:S(2)}, u32[]{:S(2)}) collective-permute-start(bf16[256,1152]{1,0:T(8,128)(2,1)S(1)} %get-tuple-element.20), channel_id=1, source_target_pairs={{0,1008},{1,17},{2,1010},{3,19},{4,1012},{5,21},{6,1014},{7,23},{8... | collective-permute-start | bytes 1769480 | tf_op jit(solution)/shard_map/ppermute | solution.py:31
  164.1 87.2 %collective-permute-start.4 = (f32[256]{0:T(256)S(1)}, f32[256]{0:T(256)S(1)}, u32[]{:S(2)}, u32[]{:S(2)}) collective-permute-start(f32[256]{0:T(256)S(1)} %reduce.1), channel_id=1, source_target_pairs={{0,16},{1,1009},{2,18},{3,1011},{4,20},{5,1013},{6,22},{7,1015},{8... | collective-permute-start | bytes 3080 | tf_op jit(solution)/shard_map/ppermute | solution.py:31

commit v3 on v2

v3 whole, which is shorter than its diff:
```python
import jax
import jax.numpy as jnp
from jax import lax
from jax.experimental import pallas as pl
from jax.experimental.pallas import tpu as pltpu
from jax.sharding import PartitionSpec as P

def paired(b, n):
    return b ^ 1


def crossed(b, n):
    return (b - 1 if b % 2 == 0 else b + 1) % n


def ring_out(b, n):
    return (b - 4 if b % 2 == 0 else b + 4) % n


def ring_back(b, n):
    return (b + 4 if b % 2 == 0 else b - 4) % n


def move(block, even, odd):
    n_blk, n_grp = lax.axis_size("blk"), lax.axis_size("grp")
    route = [
        (b * n_grp + g, (odd if g % 2 else even)(b, n_blk) * n_grp + g)
        for b in range(n_blk)
        for g in range(n_grp)
    ]
    return lax.ppermute(block, ("blk", "grp"), route)


def everywhere(block, target):
    return move(block, target, target)


def normalize(ref):
    wide = ref[...].astype(jnp.float32)
    inv = lax.rsqrt(jnp.sum(wide * wide, axis=-1, keepdims=True) + 1e-06)
    unit = wide * inv
    return inv, unit, unit.astype(jnp.bfloat16)


def project(inv, unit, grad):
    return inv * (grad - unit * jnp.sum(unit * grad, axis=-1, keepdims=True))


def dot_nt(a, b):
    return lax.dot_general(a, b, (((1,), (1,)), ((), ())), preferred_element_type=jnp.float32)


def dot_nn(a, b):
    return jnp.dot(a, b, preferred_element_type=jnp.float32)


def dot_tn(a, b):
    return lax.dot_general(a, b, (((0,), (0,)), ((), ())), preferred_element_type=jnp.float32)


def pair_of(scalars, img, txt, own=False):
    logits = scalars[0] * dot_nt(img, txt) + scalars[1]
    small = jnp.exp(-jnp.abs(logits))
    part = 1.0 / (1.0 + small)
    weights = jnp.where(logits >= 0, part, small * part)
    if own:
        hit = lax.broadcasted_iota(jnp.int32, logits.shape, 0) == lax.broadcasted_iota(
            jnp.int32, logits.shape, 1
        )
        weights = jnp.where(hit, weights - 1.0, weights)
        logits = jnp.where(hit, -logits, logits)
    losses = jnp.sum(jnp.maximum(logits, 0.0) + jnp.log1p(small), axis=-1, keepdims=True)
    return losses, weights.astype(jnp.bfloat16)


def own_kernel(scalars, i0_ref, t0_ref, i0_hat, t0_hat, w00, loss00):
    _, _, i0 = normalize(i0_ref)
    _, _, t0 = normalize(t0_ref)
    i0_hat[...] = i0
    t0_hat[...] = t0
    loss00[...], w00[...] = pair_of(scalars, i0, t0, own=True)


def main_kernel(
    scalars, i0_hat, t0_hat, i1_ref, t1_ref, loss00,
    i1_hat, t1_hat, inv_i, inv_t, w01, w10, di1, dt1, loss0, loss1,
):
    inv_i[...], _, i1 = normalize(i1_ref)
    inv_t[...], _, t1 = normalize(t1_ref)
    i1_hat[...] = i1
    t1_hat[...] = t1
    i0, t0 = i0_hat[...], t0_hat[...]
    a, w01_ = pair_of(scalars, i0, t1)
    loss0[...] = loss00[...] + a
    a, w10_ = pair_of(scalars, i1, t0)
    b, w11 = pair_of(scalars, i1, t1)
    loss1[...] = a + b
    w01[...] = w01_
    w10[...] = w10_
    di1[...] = dot_nn(w10_, t0) + dot_nn(w11, t1)
    dt1[...] = dot_tn(w01_, i0) + dot_tn(w11, i1)


def rest_kernel(
    scalars, i1_ref, t1_ref, i1_hat, t1_hat, inv_i, inv_t, ir_ref, tr_ref, di1, dt1, loss1,
    first, second, loss,
):
    scale, odd = scalars[0], scalars[2] > 0.5
    _, _, ir = normalize(ir_ref)
    _, _, tr = normalize(tr_ref)
    i1, t1 = i1_hat[...], t1_hat[...]
    a, w1r = pair_of(scalars, i1, tr)
    loss[...] = loss1[...] + a
    _, wr1 = pair_of(scalars, ir, t1)
    gi = project(
        inv_i[...], i1_ref[...].astype(jnp.float32) * inv_i[...],
        scale * (di1[...] + dot_nn(w1r, tr)),
    )
    gt = project(
        inv_t[...], t1_ref[...].astype(jnp.float32) * inv_t[...],
        scale * (dt1[...] + dot_tn(wr1, ir)),
    )
    first[...] = jnp.where(odd, gt, gi).astype(jnp.bfloat16)
    second[...] = jnp.where(odd, gi, gt).astype(jnp.bfloat16)


def home_kernel(
    scalars, i0_ref, t0_ref, i0_hat, t0_hat, i1_hat, t1_hat, w00, w01, w10, after, gi0, gt0
):
    scale = scalars[0]
    inv_i, unit_i, _ = normalize(i0_ref)
    inv_t, unit_t, _ = normalize(t0_ref)
    i0, t0, i1, t1 = i0_hat[...], t0_hat[...], i1_hat[...], t1_hat[...]
    gi0[...] = project(inv_i, unit_i, scale * (dot_nn(w00[...], t0) + dot_nn(w01[...], t1)))
    gt0[...] = project(inv_t, unit_t, scale * (dot_tn(w00[...], i0) + dot_tn(w10[...], i1)))


def sum_kernel(scalars, gi0, gt0, first, second, grad_image, grad_text):
    odd = scalars[2] > 0.5
    a, b = first[...].astype(jnp.float32), second[...].astype(jnp.float32)
    grad_image[...] = (gi0[...] + jnp.where(odd, b, a)).astype(jnp.bfloat16)
    grad_text[...] = (gt0[...] + jnp.where(odd, a, b)).astype(jnp.bfloat16)


def call(kernel, name, outs, flops, *args, steps=1):
    def spec(array):
        if steps == 1:
            return pl.BlockSpec(memory_space=pltpu.VMEM)
        return pl.BlockSpec((array.shape[0] // steps, array.shape[1]), lambda i: (i, 0))

    return pl.pallas_call(
        kernel,
        name=name,
        grid=(steps,) if steps > 1 else (),
        out_shape=outs,
        in_specs=[pl.BlockSpec(memory_space=pltpu.SMEM)] + [spec(a) for a in args[1:]],
        out_specs=[spec(a) for a in outs],
        compiler_params=pltpu.CompilerParams(vmem_limit_bytes=40 * 1024 * 1024),
        cost_estimate=pl.CostEstimate(
            flops=flops, bytes_accessed=8 * 1024 * 1024, transcendentals=0
        ),
    )(*args)


def on_device(image_embed, text_embed, log_temp, logit_bias):
    rows, wide = image_embed.shape
    odd = (lax.axis_index("grp") & 1).astype(jnp.float32)
    scalars = jnp.concatenate([jnp.exp(log_temp), logit_bias, odd[None]])
    full = jax.ShapeDtypeStruct((rows, wide), jnp.float32)
    half = jax.ShapeDtypeStruct((rows, wide), jnp.bfloat16)
    square = jax.ShapeDtypeStruct((rows, rows), jnp.bfloat16)
    column = jax.ShapeDtypeStruct((rows, 1), jnp.float32)
    product = 2 * rows * rows * wide

    i1 = everywhere(image_embed, paired)
    t1 = everywhere(text_embed, crossed)
    i0_hat, t0_hat, w00, loss00 = call(
        own_kernel, "own", [half, half, square, column], product,
        scalars, image_embed, text_embed,
    )
    i1, i0_hat = lax.optimization_barrier((i1, i0_hat))
    ir = everywhere(i1, ring_back)
    tr = everywhere(t1, ring_out)
    i1_hat, t1_hat, inv_i, inv_t, w01, w10, di1, dt1, loss0, loss1 = call(
        main_kernel, "main",
        [half, half, column, column, square, square, full, full, column, column], 7 * product,
        scalars, i0_hat, t0_hat, i1, t1, loss00,
    )
    first, second, loss1 = call(
        rest_kernel, "rest", [half, half, column], 4 * product,
        scalars, i1, t1, i1_hat, t1_hat, inv_i, inv_t, ir, tr, di1, dt1, loss1,
    )
    first = move(first, paired, crossed)
    second = move(second, crossed, paired)
    loss_in = everywhere(loss1.reshape(rows), paired)
    gi0, gt0 = call(
        home_kernel, "home", [full, full], 4 * product,
        scalars, image_embed, text_embed, i0_hat, t0_hat, i1_hat, t1_hat, w00, w01, w10, loss1,
    )
    grad_image, grad_text = call(
        sum_kernel, "total", [half, half], 4 * rows * wide,
        scalars, gi0, gt0, first, second, steps=4,
    )
    return (loss0.reshape(rows) + loss_in, grad_image, grad_text)


def solution(mesh):
    in_specs = (P(("blk", "grp"), None), P(("blk", "grp"), None), P(), P())
    out_specs = (P(("blk", "grp")), P(("blk", "grp"), None), P(("blk", "grp"), None))
    return jax.shard_map(
        on_device, mesh=mesh, in_specs=in_specs, out_specs=out_specs, check_vma=False
    )
```

time: 256 us -> 274 us (1.070)
  the two profiles are of different devices: /device:TPU:113 before, /device:TPU:64 now
where the time goes in v3:
time: 274 us; the launch traced here: 273 us
  waiting for transfers between devices  174 us (64%)
  starting transfers between devices  72.6 us (26%)
  Pallas kernels  11.3 us (4%)
  local copies, waits for them, and re-layouts  10.5 us (4%)
    ppermute x7, waiting for transfers between devices, move(): return lax.ppermute(block, ('blk', 'grp'), route)  174 us
    ppermute x7, starting transfers between devices, move(): return lax.ppermute(block, ('blk', 'grp'), route)  72.6 us
    pallas_call x5, Pallas kernels, call(): pl.pallas_call(kernel, name=name, grid=(steps,) if steps > 1 else (), out...  11.3 us
    unnamed x34, local copies, waits for them, and re-layouts  10.5 us
  transfers between devices with their start and end apart: 7, of which 5 were waited for; matrix products, arithmetic and copies ran while one was open for 1% of the time, Pallas kernels for 2%

profile of v3, /device:TPU:64, one launch (start us, length us, event | category | flops | bytes accessed | tf_op | source)
XLA Modules:
  0.0 273.4 jit_solution(8970323084801324885)
XLA Ops:
  0.6 15.7 %collective-permute-start = (bf16[256,1152]{1,0:T(8,128)(2,1)}, bf16[256,1152]{1,0:T(8,128)(2,1)S(1)}, u32[]{:S(2)}, u32[]{:S(2)}) collective-permute-start(bf16[256,1152]{1,0:T(8,128)(2,1)} %i0_ref.3), channel_id=1, source_target_pairs={{0,16},{1,17},{2,18},{3,19},{4,20},{5,21},{6,22},{7,23},{8,24},{9,... | collective-permute-start | bytes 1769480 | tf_op jit(solution)/shard_map/ppermute | solution.py:31
  16.4 18.6 %collective-permute-start.1 = (bf16[256,1152]{1,0:T(8,128)(2,1)}, bf16[256,1152]{1,0:T(8,128)(2,1)S(1)}, u32[]{:S(2)}, u32[]{:S(2)}) collective-permute-start(bf16[256,1152]{1,0:T(8,128)(2,1)} %t0_ref.3), channel_id=1, source_target_pairs={{0,1008},{1,1009},{2,1010},{3,1011},{4,1012},{5,1013},{6,1014},{7,... | collective-permute-start | bytes 1769480 | tf_op jit(solution)/shard_map/ppermute | solution.py:31
  36.3 0.1 pad_maximum_fusion.scalars
  36.4 0.0 copy-start
  36.4 1.1 copy-done
  37.4 0.0 copy-start.2
  37.4 1.1 copy-done.2
  38.5 1.4 own.1
  39.9 0.0 copy-start.10
  39.9 0.6 copy-done.10
  40.5 0.0 copy-start.4
  40.5 0.0 copy-start.6
  40.5 63.9 %collective-permute-done.i1_ref = bf16[256,1152]{1,0:T(8,128)(2,1)S(1)} collective-permute-done((bf16[256,1152]{1,0:T(8,128)(2,1)}, bf16[256,1152]{1,0:T(8,128)(2,1)S(1)}, u32[]{:S(2)}, u32[]{:S(2)}) %collective-permute-start) | collective-permute-done | bytes 589856 | tf_op jit(solution)/shard_map/ppermute | solution.py:31
  104.4 3.7 %collective-permute-start.2 = (bf16[256,1152]{1,0:T(8,128)(2,1)S(1)}, bf16[256,1152]{1,0:T(8,128)(2,1)S(1)}, u32[]{:S(2)}, u32[]{:S(2)}) collective-permute-start(bf16[256,1152]{1,0:T(8,128)(2,1)S(1)} %collective-permute-done.i1_ref), channel_id=1, source_target_pairs={{0,64},{1,65},{2,66},{3,67},{4,68},{5,69},{6,70},{7,71},{8,72},{9,... | collective-permute-start | bytes 1769480 | tf_op jit(solution)/shard_map/ppermute | solution.py:31
  108.2 24.4 %collective-permute-done.1.t1_ref = bf16[256,1152]{1,0:T(8,128)(2,1)S(1)} collective-permute-done((bf16[256,1152]{1,0:T(8,128)(2,1)}, bf16[256,1152]{1,0:T(8,128)(2,1)S(1)}, u32[]{:S(2)}, u32[]{:S(2)}) %collective-permute-start.1) | collective-permute-done | bytes 589856 | tf_op jit(solution)/shard_map/ppermute | solution.py:31
  132.6 3.8 %collective-permute-start.3 = (bf16[256,1152]{1,0:T(8,128)(2,1)S(1)}, bf16[256,1152]{1,0:T(8,128)(2,1)S(1)}, u32[]{:S(2)}, u32[]{:S(2)}) collective-permute-start(bf16[256,1152]{1,0:T(8,128)(2,1)S(1)} %collective-permute-done.1.t1_ref), channel_id=1, source_target_pairs={{0,960},{1,961},{2,962},{3,963},{4,964},{5,965},{6,966},{7,967},{8... | collective-permute-start | bytes 1769480 | tf_op jit(solution)/shard_map/ppermute | solution.py:31
  136.4 2.4 main.1
  138.8 0.0 copy-done.4
  138.8 0.0 copy-done.6
  138.8 0.0 copy-start.12
  138.8 0.6 copy-done.12
  139.5 0.0 copy-start.14
  139.5 0.6 copy-done.14
  140.1 0.0 collective-permute-done.2.ir_ref
  140.1 9.0 %collective-permute-done.3.tr_ref = bf16[256,1152]{1,0:T(8,128)(2,1)S(1)} collective-permute-done((bf16[256,1152]{1,0:T(8,128)(2,1)S(1)}, bf16[256,1152]{1,0:T(8,128)(2,1)S(1)}, u32[]{:S(2)}, u32[]{:S(2)}) %collective-permute-start.3) | collective-permute-done | bytes 589856 | tf_op jit(solution)/shard_map/ppermute | solution.py:31
  149.1 3.4 %rest.1 = (bf16[256,1152]{1,0:T(8,128)(2,1)}, bf16[256,1152]{1,0:T(8,128)(2,1)}, f32[256,1]{1,0:T(8,128)S(1)}) custom-call(f32[3]{0:T(128)S(1)} %pad_maximum_fusion.scalars, bf16[256,1152]{1,0:T(8,128)(2,1)S(1)} %collective-permute-done.i1_ref, bf16[256,1152]{1,0:T(8,128)(2,1)S(1)} %collective-permute-done.1.t1_ref, ...), custom_call_target="tpu_custom_call" | custom-call | flops 603979776 | bytes 8388608 | tf_op jit(solution)/shard_map/rest/pallas_call | solution.py:151
  152.5 0.0 copy-done.16
  152.5 0.7 copy-done.8
  153.2 1.9 collective-permute-start.5
  155.1 17.4 %collective-permute-start.6 = (bf16[256,1152]{1,0:T(8,128)(2,1)}, bf16[256,1152]{1,0:T(8,128)(2,1)S(1)}, u32[]{:S(2)}, u32[]{:S(2)}) collective-permute-start(bf16[256,1152]{1,0:T(8,128)(2,1)} %get-tuple-element.46), channel_id=1, source_target_pairs={{0,1008},{1,17},{2,1010},{3,19},{4,1012},{5,21},{6,1014},{7,23},{8... | collective-permute-start | bytes 1769480 | tf_op jit(solution)/shard_map/ppermute | solution.py:31
  172.5 1.0 reduce
  173.5 1.0 reduce.1
  174.5 11.5 %collective-permute-start.4 = (f32[256]{0:T(256)S(1)}, f32[256]{0:T(256)S(1)}, u32[]{:S(2)}, u32[]{:S(2)}) collective-permute-start(f32[256]{0:T(256)S(1)} %reduce.1), channel_id=1, source_target_pairs={{0,16},{1,17},{2,18},{3,19},{4,20},{5,21},{6,22},{7,23},{8,24},{9,... | collective-permute-start | bytes 3080 | tf_op jit(solution)/shard_map/ppermute | solution.py:31
  186.0 0.0 copy-done.1
  186.0 0.0 copy-done.3
  186.0 0.0 copy-start.5
  186.0 1.1 copy-done.5
  187.1 1.1 copy-done.7
  188.1 0.9 copy-done.9
  189.0 0.9 copy-done.11
  189.9 0.9 copy-done.13
  190.8 0.9 copy-done.15
  191.7 1.8 home.1
  193.6 72.4 %collective-permute-done.4 = f32[256]{0:T(256)S(1)} collective-permute-done((f32[256]{0:T(256)S(1)}, f32[256]{0:T(256)S(1)}, u32[]{:S(2)}, u32[]{:S(2)}) %collective-permute-start.4) | collective-permute-done | bytes 1056 | tf_op jit(solution)/shard_map/ppermute | solution.py:31
  265.9 0.6 add.3
  266.5 0.0 collective-permute-done.5.first
  266.5 4.7 %collective-permute-done.6.second = bf16[256,1152]{1,0:T(8,128)(2,1)S(1)} collective-permute-done((bf16[256,1152]{1,0:T(8,128)(2,1)}, bf16[256,1152]{1,0:T(8,128)(2,1)S(1)}, u32[]{:S(2)}, u32[]{:S(2)}) %collective-permute-start.6) | collective-permute-done | bytes 589856 | tf_op jit(solution)/shard_map/ppermute | solution.py:31
  271.2 2.2 total.1
  (9 shorter events, 0.0 us)
Async XLA Ops:
  0.6 103.8 %collective-permute-start = (bf16[256,1152]{1,0:T(8,128)(2,1)}, bf16[256,1152]{1,0:T(8,128)(2,1)S(1)}, u32[]{:S(2)}, u32[]{:S(2)}) collective-permute-start(bf16[256,1152]{1,0:T(8,128)(2,1)} %i0_ref.3), channel_id=1, source_target_pairs={{0,16},{1,17},{2,18},{3,19},{4,20},{5,21},{6,22},{7,23},{8,24},{9,... | collective-permute-start | bytes 1769480 | tf_op jit(solution)/shard_map/ppermute | solution.py:31
  16.4 116.2 %collective-permute-start.1 = (bf16[256,1152]{1,0:T(8,128)(2,1)}, bf16[256,1152]{1,0:T(8,128)(2,1)S(1)}, u32[]{:S(2)}, u32[]{:S(2)}) collective-permute-start(bf16[256,1152]{1,0:T(8,128)(2,1)} %t0_ref.3), channel_id=1, source_target_pairs={{0,1008},{1,1009},{2,1010},{3,1011},{4,1012},{5,1013},{6,1014},{7,... | collective-permute-start | bytes 1769480 | tf_op jit(solution)/shard_map/ppermute | solution.py:31
  36.4 1.1 copy-start
  37.4 1.1 copy-start.2
  39.9 0.6 copy-start.10
  40.5 98.3 %copy-start.4 = (bf16[256,1152]{1,0:T(8,128)(2,1)}, bf16[256,1152]{1,0:T(8,128)(2,1)S(1)}, u32[]{:S(2)}) copy-start(bf16[256,1152]{1,0:T(8,128)(2,1)S(1)} %get-tuple-element.27.i0_hat) | copy-start | bytes 1769476
  40.5 98.3 %copy-start.6 = (bf16[256,1152]{1,0:T(8,128)(2,1)}, bf16[256,1152]{1,0:T(8,128)(2,1)S(1)}, u32[]{:S(2)}) copy-start(bf16[256,1152]{1,0:T(8,128)(2,1)S(1)} %get-tuple-element.28.t0_hat) | copy-start | bytes 1769476
  104.4 35.7 %collective-permute-start.2 = (bf16[256,1152]{1,0:T(8,128)(2,1)S(1)}, bf16[256,1152]{1,0:T(8,128)(2,1)S(1)}, u32[]{:S(2)}, u32[]{:S(2)}) collective-permute-start(bf16[256,1152]{1,0:T(8,128)(2,1)S(1)} %collective-permute-done.i1_ref), channel_id=1, source_target_pairs={{0,64},{1,65},{2,66},{3,67},{4,68},{5,69},{6,70},{7,71},{8,72},{9,... | collective-permute-start | bytes 1769480 | tf_op jit(solution)/shard_map/ppermute | solution.py:31
  132.6 16.5 %collective-permute-start.3 = (bf16[256,1152]{1,0:T(8,128)(2,1)S(1)}, bf16[256,1152]{1,0:T(8,128)(2,1)S(1)}, u32[]{:S(2)}, u32[]{:S(2)}) collective-permute-start(bf16[256,1152]{1,0:T(8,128)(2,1)S(1)} %collective-permute-done.1.t1_ref), channel_id=1, source_target_pairs={{0,960},{1,961},{2,962},{3,963},{4,964},{5,965},{6,966},{7,967},{8... | collective-permute-start | bytes 1769480 | tf_op jit(solution)/shard_map/ppermute | solution.py:31
  138.8 0.7 copy-start.12
  139.5 0.6 copy-start.14
  140.1 12.4 %copy-start.16 = (f32[256,1]{1,0:T(8,128)}, f32[256,1]{1,0:T(8,128)S(1)}, u32[]{:S(2)}) copy-start(f32[256,1]{1,0:T(8,128)S(1)} %get-tuple-element.31) | copy-start | bytes 3076
  149.1 36.9 %copy-start.1 = (bf16[256,1152]{1,0:T(8,128)(2,1)S(1)}, bf16[256,1152]{1,0:T(8,128)(2,1)}, u32[]{:S(2)}) copy-start(bf16[256,1152]{1,0:T(8,128)(2,1)} %i0_ref.3) | copy-start | bytes 1769476
  149.1 36.9 %copy-start.3 = (bf16[256,1152]{1,0:T(8,128)(2,1)S(1)}, bf16[256,1152]{1,0:T(8,128)(2,1)}, u32[]{:S(2)}) copy-start(bf16[256,1152]{1,0:T(8,128)(2,1)} %t0_ref.3) | copy-start | bytes 1769476
  152.5 0.7 copy-start.8
  153.2 113.3 %collective-permute-start.5 = (bf16[256,1152]{1,0:T(8,128)(2,1)}, bf16[256,1152]{1,0:T(8,128)(2,1)S(1)}, u32[]{:S(2)}, u32[]{:S(2)}) collective-permute-start(bf16[256,1152]{1,0:T(8,128)(2,1)} %get-tuple-element.45), channel_id=1, source_target_pairs={{0,16},{1,1009},{2,18},{3,1011},{4,20},{5,1013},{6,22},{7,1015},{8... | collective-permute-start | bytes 1769480 | tf_op jit(solution)/shard_map/ppermute | solution.py:31
  155.1 116.1 %collective-permute-start.6 = (bf16[256,1152]{1,0:T(8,128)(2,1)}, bf16[256,1152]{1,0:T(8,128)(2,1)S(1)}, u32[]{:S(2)}, u32[]{:S(2)}) collective-permute-start(bf16[256,1152]{1,0:T(8,128)(2,1)} %get-tuple-element.46), channel_id=1, source_target_pairs={{0,1008},{1,17},{2,1010},{3,19},{4,1012},{5,21},{6,1014},{7,23},{8... | collective-permute-start | bytes 1769480 | tf_op jit(solution)/shard_map/ppermute | solution.py:31
  174.5 91.4 %collective-permute-start.4 = (f32[256]{0:T(256)S(1)}, f32[256]{0:T(256)S(1)}, u32[]{:S(2)}, u32[]{:S(2)}) collective-permute-start(f32[256]{0:T(256)S(1)} %reduce.1), channel_id=1, source_target_pairs={{0,16},{1,17},{2,18},{3,19},{4,20},{5,21},{6,22},{7,23},{8,24},{9,... | collective-permute-start | bytes 3080 | tf_op jit(solution)/shard_map/ppermute | solution.py:31
  186.0 1.1 copy-start.5
  187.0 1.1 copy-start.7
  188.1 0.9 copy-start.9
  189.0 0.9 copy-start.11
  189.9 0.9 copy-start.13
  190.8 0.9 copy-start.15

commit v4 on v2

--- a/solution.py
+++ b/solution.py
@@ -85,48 +85,80 @@
     return losses, weights.astype(jnp.bfloat16)
 
 
-def main_kernel(scalars, i0_ref, t0_ref, i1_ref, t1_ref, gi0, gt0, di1, dt1, loss0, loss1):
+def own_kernel(i0_ref, t0_ref, i0_hat, t0_hat):
+    _, _, i0_hat[...] = normalize(i0_ref)
+    _, _, t0_hat[...] = normalize(t0_ref)
+
+
+def main_kernel(
+    scalars, i0_hat, t0_hat, i1_ref, t1_ref, i1_hat, t1_hat, inv_i, inv_t, di1, dt1, loss1
+):
+    inv_i[...], _, i1 = normalize(i1_ref)
+    inv_t[...], _, t1 = normalize(t1_ref)
+    i1_hat[...] = i1
+    t1_hat[...] = t1
+    i0, t0 = i0_hat[...], t0_hat[...]
+    _, w01 = pair_of(scalars, i0, t1)
+    a, w11 = pair_of(scalars, i1, t1)
+    dt1[...] = dot_tn(w01, i0) + dot_tn(w11, i1)
+    b, w10 = pair_of(scalars, i1, t0)
+    loss1[...] = a + b
+    di1[...] = dot_nn(w10, t0) + dot_nn(w11, t1)
+
+
+def text_kernel(scalars, t1_ref, t1_hat, inv_t, ir_ref, dt1, gt1):
+    _, _, ir = normalize(ir_ref)
+    _, weights = pair_of(scalars, ir, t1_hat[...])
+    unit = t1_ref[...].astype(jnp.float32) * inv_t[...]
+    grad = scalars[0] * (dt1[...] + dot_tn(weights, ir))
+    gt1[...] = project(inv_t[...], unit, grad).astype(jnp.bfloat16)
+
+
+def image_kernel(scalars, i1_ref, i1_hat, inv_i, tr_ref, di1, loss1, gi1, loss):
+    _, _, tr = normalize(tr_ref)
+    losses, weights = pair_of(scalars, i1_hat[...], tr)
+    loss[...] = loss1[...] + losses
+    unit = i1_ref[...].astype(jnp.float32) * inv_i[...]
+    grad = scalars[0] * (di1[...] + dot_nn(weights, tr))
+    gi1[...] = project(inv_i[...], unit, grad).astype(jnp.bfloat16)
+
+
+def home_kernel(scalars, i0_ref, t0_ref, i1_hat, t1_hat, after, gi0, gt0, loss0):
     scale = scalars[0]
-    inv_i0, unit_i0, i0 = normalize(i0_ref)
-    inv_t0, unit_t0, t0 = normalize(t0_ref)
-    _, _, i1 = normalize(i1_ref)
-    _, _, t1 = normalize(t1_ref)
+    inv_i, unit_i, i0 = normalize(i0_ref)
+    inv_t, unit_t, t0 = normalize(t0_ref)
+    i1, t1 = i1_hat[...], t1_hat[...]
     a, w00 = pair_of(scalars, i0, t0, own=True)
     b, w01 = pair_of(scalars, i0, t1)
     loss0[...] = a + b
-    a, w10 = pair_of(scalars, i1, t0)
-    b, w11 = pair_of(scalars, i1, t1)
-    loss1[...] = a + b
-    di1[...] = dot_nn(w10, t0) + dot_nn(w11, t1)
-    dt1[...] = dot_tn(w01, i0) + dot_tn(w11, i1)
-    gi0[...] = project(inv_i0, unit_i0, scale * (dot_nn(w00, t0) + dot_nn(w01, t1)))
-    gt0[...] = project(inv_t0, unit_t0, scale * (dot_tn(w00, i0) + dot_tn(w10, i1)))
-
-
-def rest_kernel(scalars, i1_ref, t1_ref, ir_ref, tr_ref, di1, dt1, loss1, gi1, gt1, loss):
-    scale = scalars[0]
-    inv_i1, unit_i1, i1 = normalize(i1_ref)
-    inv_t1, unit_t1, t1 = normalize(t1_ref)
-    _, _, ir = normalize(ir_ref)
-    _, _, tr = normalize(tr_ref)
-    a, w1r = pair_of(scalars, i1, tr)
-    loss[...] = loss1[...] + a
-    _, wr1 = pair_of(scalars, ir, t1)
-    gi1[...] = project(inv_i1, unit_i1, scale * (di1[...] + dot_nn(w1r, tr))).astype(jnp.bfloat16)
-    gt1[...] = project(inv_t1, unit_t1, scale * (dt1[...] + dot_tn(wr1, ir))).astype(jnp.bfloat16)
-
-
-def call(kernel, name, outs, flops, *args):
-    vmem = pl.BlockSpec(memory_space=pltpu.VMEM)
+    _, w10 = pair_of(scalars, i1, t0)
+    gi0[...] = project(inv_i, unit_i, scale * (dot_nn(w00, t0) + dot_nn(w01, t1)))
+    gt0[...] = project(inv_t, unit_t, scale * (dot_tn(w00, i0) + dot_tn(w10, i1)))
+
+
+def sum_kernel(gi0, gt0, gi, gt, grad_image, grad_text):
+    grad_image[...] = (gi0[...] + gi[...].astype(jnp.float32)).astype(jnp.bfloat16)
+    grad_text[...] = (gt0[...] + gt[...].astype(jnp.float32)).astype(jnp.bfloat16)
+
+
+def call(kernel, name, outs, flops, *args, steps=1):
+    def spec(array):
+        if array.ndim == 1:
+            return pl.BlockSpec(memory_space=pltpu.SMEM)
+        if steps == 1:
+            return pl.BlockSpec(memory_space=pltpu.VMEM)
+        return pl.BlockSpec((array.shape[0] // steps, array.shape[1]), lambda i: (i, 0))
+
     return pl.pallas_call(
         kernel,
         name=name,
+        grid=(steps,) if steps > 1 else (),
         out_shape=outs,
-        in_specs=[pl.BlockSpec(memory_space=pltpu.SMEM)] + [vmem] * (len(args) - 1),
-        out_specs=[vmem] * len(outs),
+        in_specs=[spec(a) for a in args],
+        out_specs=[spec(a) for a in outs],
         compiler_params=pltpu.CompilerParams(vmem_limit_bytes=40 * 1024 * 1024),
         cost_estimate=pl.CostEstimate(
-            flops=flops, bytes_accessed=8 * 1024 * 1024, transcendentals=0
+            flops=flops, bytes_accessed=4 * 1024 * 1024, transcendentals=0
         ),
     )(*args)
 
@@ -141,21 +173,32 @@
 
     i1 = swap_image(image_embed)
     t1 = swap_text(text_embed)
+    i0_hat, t0_hat = call(own_kernel, "own", [half, half], product, image_embed, text_embed)
+    i1, i0_hat, scalars = lax.optimization_barrier((i1, i0_hat, scalars))
     ir = pass_image(i1)
     tr = pass_text(t1)
-    gi0, gt0, di1, dt1, loss0, loss1 = call(
-        main_kernel, "main", [full] * 4 + [column] * 2, 12 * product,
-        scalars, image_embed, text_embed, i1, t1,
-    )
-    gi1, gt1, loss1 = call(
-        rest_kernel, "rest", [half, half, column], 4 * product,
-        scalars, i1, t1, ir, tr, di1, dt1, loss1,
+    i1_hat, t1_hat, inv_i, inv_t, di1, dt1, loss1 = call(
+        main_kernel, "main", [half, half, column, column, full, full, column], 7 * product,
+        scalars, i0_hat, t0_hat, i1, t1,
+    )
+    (gt1,) = call(
+        text_kernel, "text_share", [half], 2 * product,
+        scalars, t1, t1_hat, inv_t, ir, dt1,
+    )
+    gt = swap_text(gt1)
+    gi1, loss1 = call(
+        image_kernel, "image_share", [half, column], 2 * product,
+        scalars, i1, i1_hat, inv_i, tr, di1, loss1,
     )
     gi = swap_image(gi1)
-    gt = swap_text(gt1)
     loss_in = swap_image(loss1.reshape(rows))
-    grad_image = (gi0 + gi.astype(jnp.float32)).astype(jnp.bfloat16)
-    grad_text = (gt0 + gt.astype(jnp.float32)).astype(jnp.bfloat16)
+    gi0, gt0, loss0 = call(
+        home_kernel, "home", [full, full, column], 7 * product,
+        scalars, image_embed, text_embed, i1_hat, t1_hat, loss1,
+    )
+    grad_image, grad_text = call(
+        sum_kernel, "total", [half, half], 4 * rows * wide, gi0, gt0, gi, gt, steps=4
+    )
     return (loss0.reshape(rows) + loss_in, grad_image, grad_text)
 
 

time: 256 us -> 259 us (1.012)
  the two profiles are of different devices: /device:TPU:113 before, /device:TPU:33 now
where the time goes in v4:
time: 259 us; the launch traced here: 258 us
  waiting for transfers between devices  158 us (61%)
  starting transfers between devices  75.5 us (29%)
  Pallas kernels  12.8 us (5%)
  local copies, waits for them, and re-layouts  7.94 us (3%)
    ppermute x7, waiting for transfers between devices, move(): return lax.ppermute(block, ('blk', 'grp'), route)  158 us
    ppermute x7, starting transfers between devices, move(): return lax.ppermute(block, ('blk', 'grp'), route)  75.5 us
    pallas_call x6, Pallas kernels, call(): pl.pallas_call(kernel, name=name, grid=(steps,) if steps > 1 else (), out...  12.8 us
    unnamed x22, local copies, waits for them, and re-layouts  7.94 us
  transfers between devices with their start and end apart: 7, of which 3 were waited for; matrix products, arithmetic and copies ran while one was open for 1% of the time, Pallas kernels for 4%

profile of v4, /device:TPU:33, one launch (start us, length us, event | category | flops | bytes accessed | tf_op | source)
XLA Modules:
  0.0 258.2 jit_solution(2454754218676832876)
XLA Ops:
  0.6 26.5 %collective-permute-start = (bf16[256,1152]{1,0:T(8,128)(2,1)}, bf16[256,1152]{1,0:T(8,128)(2,1)S(1)}, u32[]{:S(2)}, u32[]{:S(2)}) collective-permute-start(bf16[256,1152]{1,0:T(8,128)(2,1)} %i0_ref.3), channel_id=1, source_target_pairs={{0,16},{1,1009},{2,18},{3,1011},{4,20},{5,1013},{6,22},{7,1015},{8... | collective-permute-start | bytes 1769480 | tf_op jit(solution)/shard_map/ppermute | solution.py:31
  27.1 3.5 %collective-permute-start.1 = (bf16[256,1152]{1,0:T(8,128)(2,1)}, bf16[256,1152]{1,0:T(8,128)(2,1)S(1)}, u32[]{:S(2)}, u32[]{:S(2)}) collective-permute-start(bf16[256,1152]{1,0:T(8,128)(2,1)} %t0_ref.3), channel_id=1, source_target_pairs={{0,1008},{1,17},{2,1010},{3,19},{4,1012},{5,21},{6,1014},{7,23},{8... | collective-permute-start | bytes 1769480 | tf_op jit(solution)/shard_map/ppermute | solution.py:31
  32.0 0.0 copy-start
  32.0 1.1 copy-done
  33.0 0.0 copy-start.2
  33.0 1.1 copy-done.2
  34.1 0.4 own.1
  34.5 0.1 pad_maximum_fusion.scalars
  34.5 76.4 %collective-permute-done.i1_ref = bf16[256,1152]{1,0:T(8,128)(2,1)S(1)} collective-permute-done((bf16[256,1152]{1,0:T(8,128)(2,1)}, bf16[256,1152]{1,0:T(8,128)(2,1)S(1)}, u32[]{:S(2)}, u32[]{:S(2)}) %collective-permute-start) | collective-permute-done | bytes 589856 | tf_op jit(solution)/shard_map/ppermute | solution.py:31
  110.9 6.6 %collective-permute-start.5 = (bf16[256,1152]{1,0:T(8,128)(2,1)S(1)}, bf16[256,1152]{1,0:T(8,128)(2,1)S(1)}, u32[]{:S(2)}, u32[]{:S(2)}) collective-permute-start(bf16[256,1152]{1,0:T(8,128)(2,1)S(1)} %collective-permute-done.i1_ref), channel_id=1, source_target_pairs={{0,64},{1,961},{2,66},{3,963},{4,68},{5,965},{6,70},{7,967},{8,72}... | collective-permute-start | bytes 1769480 | tf_op jit(solution)/shard_map/ppermute | solution.py:31
  117.6 0.0 collective-permute-done.1.t1_ref
  117.6 1.9 collective-permute-start.2
  119.5 2.8 %main.1 = (bf16[256,1152]{1,0:T(8,128)(2,1)S(1)}, bf16[256,1152]{1,0:T(8,128)(2,1)S(1)}, f32[256,1]{1,0:T(8,128)S(1)}, f32[256,1]{1,0:T(8,128)S(1)}, f32[256,115...) custom-call(f32[2]{0:T(128)S(1)} %pad_maximum_fusion.scalars, ...), custom_call_target="tpu_custom_call" | custom-call | flops 1056964608 | bytes 4194304 | tf_op jit(solution)/shard_map/main/pallas_call | solution.py:152
  122.3 0.0 copy-start.6
  122.3 0.0 copy-start.4
  122.3 2.0 collective-permute-done.5.ir_ref
  124.4 2.7 %text_share.1 = bf16[256,1152]{1,0:T(8,128)(2,1)} custom-call(f32[2]{0:T(128)S(1)} %pad_maximum_fusion.scalars, bf16[256,1152]{1,0:T(8,128)(2,1)S(1)} %collective-permute-done.1.t1_ref, bf16[256,1152]{1,0:T(8,128)(2,1)S(1)} %get-tuple-element.28.t1_hat, f32[256,1]{1,0:T(8,128)S(1)} %get-tuple-element.37.inv_t, ...), custom_call_target="tpu_custom_call" | custom-call | flops 301989888 | bytes 4194304 | tf_op jit(solution)/shard_map/text_share/pallas_call | solution.py:152
  127.1 0.0 copy-done.6
  127.1 18.8 %collective-permute-start.6 = (bf16[256,1152]{1,0:T(8,128)(2,1)}, bf16[256,1152]{1,0:T(8,128)(2,1)S(1)}, u32[]{:S(2)}, u32[]{:S(2)}) collective-permute-start(bf16[256,1152]{1,0:T(8,128)(2,1)} %text_share.1), channel_id=1, source_target_pairs={{0,1008},{1,17},{2,1010},{3,19},{4,1012},{5,21},{6,1014},{7,23},{8... | collective-permute-start | bytes 1769480 | tf_op jit(solution)/shard_map/ppermute | solution.py:31
  145.9 0.0 collective-permute-done.2.tr_ref
  145.9 0.0 copy-done.4
  145.9 2.7 %image_share.1 = (bf16[256,1152]{1,0:T(8,128)(2,1)}, f32[256,1]{1,0:T(8,128)S(1)}) custom-call(f32[2]{0:T(128)S(1)} %pad_maximum_fusion.scalars, bf16[256,1152]{1,0:T(8,128)(2,1)S(1)} %collective-permute-done.i1_ref, bf16[256,1152]{1,0:T(8,128)(2,1)S(1)} %get-tuple-element.27.i1_hat, f32[256,1]{1,0:T(8,128)S(1)} %get-tuple-element.29.inv_i, ...), custom_call_target="tpu_custom_call" | custom-call | flops 301989888 | bytes 4194304 | tf_op jit(solution)/shard_map/image_share/pallas_call | solution.py:152
  148.6 0.0 copy-start.8
  148.6 12.4 %collective-permute-start.4 = (bf16[256,1152]{1,0:T(8,128)(2,1)}, bf16[256,1152]{1,0:T(8,128)(2,1)S(1)}, u32[]{:S(2)}, u32[]{:S(2)}) collective-permute-start(bf16[256,1152]{1,0:T(8,128)(2,1)} %get-tuple-element.36), channel_id=1, source_target_pairs={{0,16},{1,1009},{2,18},{3,1011},{4,20},{5,1013},{6,22},{7,1015},{8... | collective-permute-start | bytes 1769480 | tf_op jit(solution)/shard_map/ppermute | solution.py:31
  161.0 0.1 reduce.1
  161.1 0.0 copy-done.8
  161.1 5.8 %collective-permute-start.3 = (f32[256]{0:T(256)S(1)}, f32[256]{0:T(256)S(1)}, u32[]{:S(2)}, u32[]{:S(2)}) collective-permute-start(f32[256]{0:T(256)S(1)} %reduce.1), channel_id=1, source_target_pairs={{0,16},{1,1009},{2,18},{3,1011},{4,20},{5,1013},{6,22},{7,1015},{8... | collective-permute-start | bytes 3080 | tf_op jit(solution)/shard_map/ppermute | solution.py:31
  166.9 0.0 copy-start.1
  166.9 1.1 copy-done.1
  168.0 0.0 copy-start.3
  168.0 1.1 copy-done.3
  169.1 0.0 copy-start.5
  169.1 1.1 copy-done.5
  170.1 0.0 copy-start.7
  170.1 1.1 copy-done.7
  171.2 0.0 copy-start.9
  171.2 0.9 copy-done.9
  172.1 2.7 %home.1 = (f32[256,1152]{1,0:T(8,128)S(1)}, f32[256,1152]{1,0:T(8,128)S(1)}, f32[256,1]{1,0:T(8,128)S(1)}) custom-call(f32[2]{0:T(128)S(1)} %pad_maximum_fusion.scalars, bf16[256,1152]{1,0:T(8,128)(2,1)S(1)} %copy-done.1, bf16[256,1152]{1,0:T(8,128)(2,1)S(1)} %copy-done.3, bf16[256,1152]{1,0:T(8,128)(2,1)S(1)} %copy-done.5, bf16[256,1152]{1,0:T(8,128)(2,1)S(1)} %copy-done.7, ...), custom_call_target="tpu_custom_call" | custom-call | flops 1056964608 | bytes 4194304 | tf_op jit(solution)/shard_map/home/pallas_call | solution.py:152
  174.8 0.0 copy-start.10
  174.8 0.6 copy-done.10
  175.4 1.0 reduce
  176.4 79.6 %collective-permute-done.3 = f32[256]{0:T(256)S(1)} collective-permute-done((f32[256]{0:T(256)S(1)}, f32[256]{0:T(256)S(1)}, u32[]{:S(2)}, u32[]{:S(2)}) %collective-permute-start.3) | collective-permute-done | bytes 1056 | tf_op jit(solution)/shard_map/ppermute | solution.py:31
  256.0 0.6 add.3
  256.6 0.0 collective-permute-done.6.gt
  256.6 0.0 collective-permute-done.4.gi
  256.6 1.6 total.1
Async XLA Ops:
  0.6 110.3 %collective-permute-start = (bf16[256,1152]{1,0:T(8,128)(2,1)}, bf16[256,1152]{1,0:T(8,128)(2,1)S(1)}, u32[]{:S(2)}, u32[]{:S(2)}) collective-permute-start(bf16[256,1152]{1,0:T(8,128)(2,1)} %i0_ref.3), channel_id=1, source_target_pairs={{0,16},{1,1009},{2,18},{3,1011},{4,20},{5,1013},{6,22},{7,1015},{8... | collective-permute-start | bytes 1769480 | tf_op jit(solution)/shard_map/ppermute | solution.py:31
  27.1 90.5 %collective-permute-start.1 = (bf16[256,1152]{1,0:T(8,128)(2,1)}, bf16[256,1152]{1,0:T(8,128)(2,1)S(1)}, u32[]{:S(2)}, u32[]{:S(2)}) collective-permute-start(bf16[256,1152]{1,0:T(8,128)(2,1)} %t0_ref.3), channel_id=1, source_target_pairs={{0,1008},{1,17},{2,1010},{3,19},{4,1012},{5,21},{6,1014},{7,23},{8... | collective-permute-start | bytes 1769480 | tf_op jit(solution)/shard_map/ppermute | solution.py:31
  32.0 1.1 copy-start
  33.0 1.1 copy-start.2
  110.9 13.4 %collective-permute-start.5 = (bf16[256,1152]{1,0:T(8,128)(2,1)S(1)}, bf16[256,1152]{1,0:T(8,128)(2,1)S(1)}, u32[]{:S(2)}, u32[]{:S(2)}) collective-permute-start(bf16[256,1152]{1,0:T(8,128)(2,1)S(1)} %collective-permute-done.i1_ref), channel_id=1, source_target_pairs={{0,64},{1,961},{2,66},{3,963},{4,68},{5,965},{6,70},{7,967},{8,72}... | collective-permute-start | bytes 1769480 | tf_op jit(solution)/shard_map/ppermute | solution.py:31
  117.6 28.3 %collective-permute-start.2 = (bf16[256,1152]{1,0:T(8,128)(2,1)S(1)}, bf16[256,1152]{1,0:T(8,128)(2,1)S(1)}, u32[]{:S(2)}, u32[]{:S(2)}) collective-permute-start(bf16[256,1152]{1,0:T(8,128)(2,1)S(1)} %collective-permute-done.1.t1_ref), channel_id=1, source_target_pairs={{0,960},{1,65},{2,962},{3,67},{4,964},{5,69},{6,966},{7,71},{8,968... | collective-permute-start | bytes 1769480 | tf_op jit(solution)/shard_map/ppermute | solution.py:31
  122.3 4.8 %copy-start.6 = (bf16[256,1152]{1,0:T(8,128)(2,1)}, bf16[256,1152]{1,0:T(8,128)(2,1)S(1)}, u32[]{:S(2)}) copy-start(bf16[256,1152]{1,0:T(8,128)(2,1)S(1)} %get-tuple-element.28.t1_hat) | copy-start | bytes 1769476
  122.3 23.6 %copy-start.4 = (bf16[256,1152]{1,0:T(8,128)(2,1)}, bf16[256,1152]{1,0:T(8,128)(2,1)S(1)}, u32[]{:S(2)}) copy-start(bf16[256,1152]{1,0:T(8,128)(2,1)S(1)} %get-tuple-element.27.i1_hat) | copy-start | bytes 1769476
  127.1 129.5 %collective-permute-start.6 = (bf16[256,1152]{1,0:T(8,128)(2,1)}, bf16[256,1152]{1,0:T(8,128)(2,1)S(1)}, u32[]{:S(2)}, u32[]{:S(2)}) collective-permute-start(bf16[256,1152]{1,0:T(8,128)(2,1)} %text_share.1), channel_id=1, source_target_pairs={{0,1008},{1,17},{2,1010},{3,19},{4,1012},{5,21},{6,1014},{7,23},{8... | collective-permute-start | bytes 1769480 | tf_op jit(solution)/shard_map/ppermute | solution.py:31
  148.6 12.5 %copy-start.8 = (f32[256,1]{1,0:T(8,128)}, f32[256,1]{1,0:T(8,128)S(1)}, u32[]{:S(2)}) copy-start(f32[256,1]{1,0:T(8,128)S(1)} %get-tuple-element.32.after) | copy-start | bytes 3076
  148.6 108.0 %collective-permute-start.4 = (bf16[256,1152]{1,0:T(8,128)(2,1)}, bf16[256,1152]{1,0:T(8,128)(2,1)S(1)}, u32[]{:S(2)}, u32[]{:S(2)}) collective-permute-start(bf16[256,1152]{1,0:T(8,128)(2,1)} %get-tuple-element.36), channel_id=1, source_target_pairs={{0,16},{1,1009},{2,18},{3,1011},{4,20},{5,1013},{6,22},{7,1015},{8... | collective-permute-start | bytes 1769480 | tf_op jit(solution)/shard_map/ppermute | solution.py:31
  161.1 94.9 %collective-permute-start.3 = (f32[256]{0:T(256)S(1)}, f32[256]{0:T(256)S(1)}, u32[]{:S(2)}, u32[]{:S(2)}) collective-permute-start(f32[256]{0:T(256)S(1)} %reduce.1), channel_id=1, source_target_pairs={{0,16},{1,1009},{2,18},{3,1011},{4,20},{5,1013},{6,22},{7,1015},{8... | collective-permute-start | bytes 3080 | tf_op jit(solution)/shard_map/ppermute | solution.py:31
  166.9 1.1 copy-start.1
  168.0 1.1 copy-start.3
  169.1 1.1 copy-start.5
  170.1 1.1 copy-start.7
  171.2 0.9 copy-start.9
  174.8 0.7 copy-start.10

commit v5 on v4

--- a/solution.py
+++ b/solution.py
@@ -5,6 +5,10 @@
 from jax.experimental.pallas import tpu as pltpu
 from jax.sharding import PartitionSpec as P
 
+EXTRA = 8
+PIECES = 3
+
+
 def paired(b, n):
     return b ^ 1
 
@@ -24,7 +28,7 @@
 def move(block, even, odd):
     n_blk, n_grp = lax.axis_size("blk"), lax.axis_size("grp")
     route = [
-        (b * n_grp + g, (odd if g % 2 else even)(b, n_blk) * n_grp + g)
+        (b * n_grp + g, (odd if (g + (g + 2) // 4) % 2 else even)(b, n_blk) * n_grp + g)
         for b in range(n_blk)
         for g in range(n_grp)
     ]
@@ -114,16 +118,28 @@
     gt1[...] = project(inv_t[...], unit, grad).astype(jnp.bfloat16)
 
 
-def image_kernel(scalars, i1_ref, i1_hat, inv_i, tr_ref, di1, loss1, gi1, loss):
+def image_kernel(scalars, i1_ref, i1_hat, inv_i, tr_ref, di1, loss1, gi1):
+    rows = i1_ref.shape[0]
     _, _, tr = normalize(tr_ref)
     losses, weights = pair_of(scalars, i1_hat[...], tr)
-    loss[...] = loss1[...] + losses
+    rest, lane = loss1[...] + losses, lax.broadcasted_iota(jnp.int32, (rows, 128), 1)
+    packed = jnp.zeros((rows, 128), jnp.float32)
+    for k in range(PIECES):
+        piece = rest.astype(jnp.bfloat16).astype(jnp.float32)
+        packed = jnp.where(lane == k, piece, packed)
+        rest = rest - piece
+    hit = lax.broadcasted_iota(jnp.int32, (rows, rows), 0) == lax.broadcasted_iota(
+        jnp.int32, (rows, rows), 1
+    )
+    lines = dot_tn(packed.astype(jnp.bfloat16), hit.astype(jnp.bfloat16))
+    gi1[rows:, :] = jnp.zeros((EXTRA, gi1.shape[1]), jnp.bfloat16)
+    gi1[rows:, :rows] = lines[:EXTRA].astype(jnp.bfloat16)
     unit = i1_ref[...].astype(jnp.float32) * inv_i[...]
     grad = scalars[0] * (di1[...] + dot_nn(weights, tr))
-    gi1[...] = project(inv_i[...], unit, grad).astype(jnp.bfloat16)
-
-
-def home_kernel(scalars, i0_ref, t0_ref, i1_hat, t1_hat, after, gi0, gt0, loss0):
+    gi1[:rows, :] = project(inv_i[...], unit, grad).astype(jnp.bfloat16)
+
+
+def home_kernel(scalars, i0_ref, t0_ref, i1_hat, t1_hat, gi0, gt0, loss0):
     scale = scalars[0]
     inv_i, unit_i, i0 = normalize(i0_ref)
     inv_t, unit_t, t0 = normalize(t0_ref)
@@ -147,7 +163,7 @@
             return pl.BlockSpec(memory_space=pltpu.SMEM)
         if steps == 1:
             return pl.BlockSpec(memory_space=pltpu.VMEM)
-        return pl.BlockSpec((array.shape[0] // steps, array.shape[1]), lambda i: (i, 0))
+        return pl.BlockSpec((outs[0].shape[0] // steps, array.shape[1]), lambda i: (i, 0))
 
     return pl.pallas_call(
         kernel,
@@ -174,7 +190,7 @@
     i1 = swap_image(image_embed)
     t1 = swap_text(text_embed)
     i0_hat, t0_hat = call(own_kernel, "own", [half, half], product, image_embed, text_embed)
-    i1, i0_hat, scalars = lax.optimization_barrier((i1, i0_hat, scalars))
+    t1, i0_hat, scalars = lax.optimization_barrier((t1, i0_hat, scalars))
     ir = pass_image(i1)
     tr = pass_text(t1)
     i1_hat, t1_hat, inv_i, inv_t, di1, dt1, loss1 = call(
@@ -186,20 +202,22 @@
         scalars, t1, t1_hat, inv_t, ir, dt1,
     )
     gt = swap_text(gt1)
-    gi1, loss1 = call(
-        image_kernel, "image_share", [half, column], 2 * product,
+    taller = jax.ShapeDtypeStruct((rows + EXTRA, wide), jnp.bfloat16)
+    (gi1,) = call(
+        image_kernel, "image_share", [taller], 2 * product,
         scalars, i1, i1_hat, inv_i, tr, di1, loss1,
     )
     gi = swap_image(gi1)
-    loss_in = swap_image(loss1.reshape(rows))
+    i1_hat, gi1 = lax.optimization_barrier((i1_hat, gi1))
     gi0, gt0, loss0 = call(
         home_kernel, "home", [full, full, column], 7 * product,
-        scalars, image_embed, text_embed, i1_hat, t1_hat, loss1,
+        scalars, image_embed, text_embed, i1_hat, t1_hat,
     )
     grad_image, grad_text = call(
         sum_kernel, "total", [half, half], 4 * rows * wide, gi0, gt0, gi, gt, steps=4
     )
-    return (loss0.reshape(rows) + loss_in, grad_image, grad_text)
+    lines = gi[rows : rows + PIECES, :rows].astype(jnp.float32)
+    return (loss0.reshape(rows) + jnp.sum(lines, axis=0), grad_image, grad_text)
 
 
 def solution(mesh):

time: 259 us -> 252 us (0.973)
  local copies, waits for them, and re-layouts: 7.94 us -> 2.14 us
  starting transfers between devices: 75.5 us -> 71.8 us
    unnamed x22 -> x8, local copies, waits for them, and re-layouts: 7.94 us -> 2.14 us
    ppermute x7 -> x6, starting transfers between devices: 75.5 us -> 71.8 us  [move(): return lax.ppermute(block, ('blk', 'grp'), route)]
    ppermute x7 -> x6, waiting for transfers between devices: 158 us -> 160 us  [move(): return lax.ppermute(block, ('blk', 'grp'), route)]
  transfers between devices with their start and end apart: 7 -> 6, of which waited for: 3 -> 4; matrix products, arithmetic and copies ran while one was open for 1% -> 0% of each run, Pallas kernels for 4% -> 5%
where the time goes in v5:
time: 252 us
  waiting for transfers between devices  160 us (63%)
  starting transfers between devices  71.8 us (28%)
  Pallas kernels  15.1 us (6%)
    ppermute x6, waiting for transfers between devices, move(): return lax.ppermute(block, ('blk', 'grp'), route)  160 us
    ppermute x6, starting transfers between devices, move(): return lax.ppermute(block, ('blk', 'grp'), route)  71.8 us
    pallas_call x6, Pallas kernels, call(): pl.pallas_call(kernel, name=name, grid=(steps,) if steps > 1 else (), out...  15.1 us
  transfers between devices with their start and end apart: 6, of which 4 were waited for; matrix products, arithmetic and copies ran while one was open for 0% of the time, Pallas kernels for 5%

profile of v5, /device:TPU:33, one launch (start us, length us, event | category | flops | bytes accessed | tf_op | source)
XLA Modules:
  0.0 251.6 jit_solution(2705929442832506403)
XLA Ops:
  0.6 26.5 %collective-permute-start = (bf16[256,1152]{1,0:T(8,128)(2,1)}, bf16[256,1152]{1,0:T(8,128)(2,1)S(1)}, u32[]{:S(2)}, u32[]{:S(2)}) collective-permute-start(bf16[256,1152]{1,0:T(8,128)(2,1)} %t0_ref.3), channel_id=1, source_target_pairs={{0,1008},{1,17},{2,18},{3,1011},{4,20},{5,1013},{6,1014},{7,23},{8... | collective-permute-start | bytes 1769480 | tf_op jit(solution)/shard_map/ppermute | solution.py:35
  27.1 3.5 %collective-permute-start.1 = (bf16[256,1152]{1,0:T(8,128)(2,1)}, bf16[256,1152]{1,0:T(8,128)(2,1)S(1)}, u32[]{:S(2)}, u32[]{:S(2)}) collective-permute-start(bf16[256,1152]{1,0:T(8,128)(2,1)} %i0_ref.3), channel_id=1, source_target_pairs={{0,16},{1,1009},{2,1010},{3,19},{4,1012},{5,21},{6,22},{7,1015},{8... | collective-permute-start | bytes 1769480 | tf_op jit(solution)/shard_map/ppermute | solution.py:35
  32.0 0.0 copy-start
  32.0 1.1 copy-done
  33.0 0.0 copy-start.2
  33.0 1.1 copy-done.2
  34.1 0.4 own.1
  34.5 0.1 pad_maximum_fusion.scalars
  34.5 76.7 %collective-permute-done.t1_ref = bf16[256,1152]{1,0:T(8,128)(2,1)S(1)} collective-permute-done((bf16[256,1152]{1,0:T(8,128)(2,1)}, bf16[256,1152]{1,0:T(8,128)(2,1)S(1)}, u32[]{:S(2)}, u32[]{:S(2)}) %collective-permute-start) | collective-permute-done | bytes 589856 | tf_op jit(solution)/shard_map/ppermute | solution.py:35
  111.3 6.2 %collective-permute-start.2 = (bf16[256,1152]{1,0:T(8,128)(2,1)S(1)}, bf16[256,1152]{1,0:T(8,128)(2,1)S(1)}, u32[]{:S(2)}, u32[]{:S(2)}) collective-permute-start(bf16[256,1152]{1,0:T(8,128)(2,1)S(1)} %collective-permute-done.t1_ref), channel_id=1, source_target_pairs={{0,960},{1,65},{2,66},{3,963},{4,68},{5,965},{6,966},{7,71},{8,968... | collective-permute-start | bytes 1769480 | tf_op jit(solution)/shard_map/ppermute | solution.py:35
  117.5 0.0 collective-permute-done.1.i1_ref
  117.5 1.9 collective-permute-start.4
  119.4 2.8 %main.1 = (bf16[256,1152]{1,0:T(8,128)(2,1)S(1)}, bf16[256,1152]{1,0:T(8,128)(2,1)S(1)}, f32[256,1]{1,0:T(8,128)S(1)}, f32[256,1]{1,0:T(8,128)S(1)}, f32[256,115...) custom-call(f32[2]{0:T(128)S(1)} %pad_maximum_fusion.scalars, ...), custom_call_target="tpu_custom_call" | custom-call | flops 1056964608 | bytes 4194304 | tf_op jit(solution)/shard_map/main/pallas_call | solution.py:168
  122.3 2.0 collective-permute-done.2.tr_ref
  124.3 3.1 %image_share.1 = bf16[264,1152]{1,0:T(8,128)(2,1)} custom-call(f32[2]{0:T(128)S(1)} %pad_maximum_fusion.scalars, bf16[256,1152]{1,0:T(8,128)(2,1)S(1)} %collective-permute-done.1.i1_ref, bf16[256,1152]{1,0:T(8,128)(2,1)S(1)} %get-tuple-element.30.i1_hat, f32[256,1]{1,0:T(8,128)S(1)} %get-tuple-element.27.inv_i, ...), custom_call_target="tpu_custom_call" | custom-call | flops 301989888 | bytes 4194304 | tf_op jit(solution)/shard_map/image_share/pallas_call | solution.py:168
  127.5 20.8 %collective-permute-start.3 = (bf16[264,1152]{1,0:T(8,128)(2,1)}, bf16[264,1152]{1,0:T(8,128)(2,1)S(1)}, u32[]{:S(2)}, u32[]{:S(2)}) collective-permute-start(bf16[264,1152]{1,0:T(8,128)(2,1)} %image_share.1), channel_id=1, source_target_pairs={{0,16},{1,1009},{2,1010},{3,19},{4,1012},{5,21},{6,22},{7,1015},{8... | collective-permute-start | bytes 1824776 | tf_op jit(solution)/shard_map/ppermute | solution.py:35
  148.3 0.0 collective-permute-done.4.ir_ref
  148.3 0.0 copy-start.1
  148.3 0.0 copy-start.3
  148.3 2.7 %text_share.1 = bf16[256,1152]{1,0:T(8,128)(2,1)} custom-call(f32[2]{0:T(128)S(1)} %pad_maximum_fusion.scalars, bf16[256,1152]{1,0:T(8,128)(2,1)S(1)} %collective-permute-done.t1_ref, bf16[256,1152]{1,0:T(8,128)(2,1)S(1)} %get-tuple-element.31.t1_hat, f32[256,1]{1,0:T(8,128)S(1)} %get-tuple-element.35.inv_t, ...), custom_call_target="tpu_custom_call" | custom-call | flops 301989888 | bytes 4194304 | tf_op jit(solution)/shard_map/text_share/pallas_call | solution.py:168
  151.1 12.8 %collective-permute-start.5 = (bf16[256,1152]{1,0:T(8,128)(2,1)}, bf16[256,1152]{1,0:T(8,128)(2,1)}, u32[]{:S(2)}, u32[]{:S(2)}) collective-permute-start(bf16[256,1152]{1,0:T(8,128)(2,1)} %text_share.1), channel_id=1, source_target_pairs={{0,1008},{1,17},{2,18},{3,1011},{4,20},{5,1013},{6,1014},{7,23},{8... | collective-permute-start | bytes 1769480 | tf_op jit(solution)/shard_map/ppermute | solution.py:35
  163.9 0.0 copy-done.1
  163.9 0.0 copy-done.3
  164.0 2.7 %home.1 = (f32[256,1152]{1,0:T(8,128)S(1)}, f32[256,1152]{1,0:T(8,128)S(1)}, f32[256,1]{1,0:T(8,128)S(1)}) custom-call(f32[2]{0:T(128)S(1)} %pad_maximum_fusion.scalars, bf16[256,1152]{1,0:T(8,128)(2,1)S(1)} %copy-done.1, bf16[256,1152]{1,0:T(8,128)(2,1)S(1)} %copy-done.3, bf16[256,1152]{1,0:T(8,128)(2,1)S(1)} %get-tuple-element.30.i1_hat, ...), custom_call_target="tpu_custom_call" | custom-call | flops 1056964608 | bytes 4194304 | tf_op jit(solution)/shard_map/home/pallas_call | solution.py:168
  166.7 0.1 reduce
  166.8 54.9 %collective-permute-done.3.gi = bf16[264,1152]{1,0:T(8,128)(2,1)S(1)} collective-permute-done((bf16[264,1152]{1,0:T(8,128)(2,1)}, bf16[264,1152]{1,0:T(8,128)(2,1)S(1)}, u32[]{:S(2)}, u32[]{:S(2)}) %collective-permute-start.3) | collective-permute-done | bytes 608288 | tf_op jit(solution)/shard_map/ppermute | solution.py:35
  221.7 0.6 add.3
  222.3 26.0 %collective-permute-done.5.gt = bf16[256,1152]{1,0:T(8,128)(2,1)} collective-permute-done((bf16[256,1152]{1,0:T(8,128)(2,1)}, bf16[256,1152]{1,0:T(8,128)(2,1)}, u32[]{:S(2)}, u32[]{:S(2)}) %collective-permute-start.5) | collective-permute-done | bytes 589856 | tf_op jit(solution)/shard_map/ppermute | solution.py:35
  248.2 3.3 %total.1 = (bf16[256,1152]{1,0:T(8,128)(2,1)}, bf16[256,1152]{1,0:T(8,128)(2,1)}) custom-call(f32[256,1152]{1,0:T(8,128)S(1)} %get-tuple-element.33.gi0, f32[256,1152]{1,0:T(8,128)S(1)} %get-tuple-element.34.gt0, bf16[264,1152]{1,0:T(8,128)(2,1)S(1)} %collective-permute-done.3.gi, bf16[256,1152]{1,0:T(8,128)(2,1)} %collective-permute-done.5.gt), custom_call_target="tpu_custom_call" | custom-call | flops 1179648 | bytes 4194304 | tf_op jit(solution)/shard_map/total/pallas_call | solution.py:168
  (1 shorter events, 0.0 us)
Async XLA Ops:
  0.6 110.6 %collective-permute-start = (bf16[256,1152]{1,0:T(8,128)(2,1)}, bf16[256,1152]{1,0:T(8,128)(2,1)S(1)}, u32[]{:S(2)}, u32[]{:S(2)}) collective-permute-start(bf16[256,1152]{1,0:T(8,128)(2,1)} %t0_ref.3), channel_id=1, source_target_pairs={{0,1008},{1,17},{2,18},{3,1011},{4,20},{5,1013},{6,1014},{7,23},{8... | collective-permute-start | bytes 1769480 | tf_op jit(solution)/shard_map/ppermute | solution.py:35
  27.1 90.4 %collective-permute-start.1 = (bf16[256,1152]{1,0:T(8,128)(2,1)}, bf16[256,1152]{1,0:T(8,128)(2,1)S(1)}, u32[]{:S(2)}, u32[]{:S(2)}) collective-permute-start(bf16[256,1152]{1,0:T(8,128)(2,1)} %i0_ref.3), channel_id=1, source_target_pairs={{0,16},{1,1009},{2,1010},{3,19},{4,1012},{5,21},{6,22},{7,1015},{8... | collective-permute-start | bytes 1769480 | tf_op jit(solution)/shard_map/ppermute | solution.py:35
  32.0 1.1 copy-start
  33.0 1.1 copy-start.2
  111.3 13.0 %collective-permute-start.2 = (bf16[256,1152]{1,0:T(8,128)(2,1)S(1)}, bf16[256,1152]{1,0:T(8,128)(2,1)S(1)}, u32[]{:S(2)}, u32[]{:S(2)}) collective-permute-start(bf16[256,1152]{1,0:T(8,128)(2,1)S(1)} %collective-permute-done.t1_ref), channel_id=1, source_target_pairs={{0,960},{1,65},{2,66},{3,963},{4,68},{5,965},{6,966},{7,71},{8,968... | collective-permute-start | bytes 1769480 | tf_op jit(solution)/shard_map/ppermute | solution.py:35
  117.5 30.8 %collective-permute-start.4 = (bf16[256,1152]{1,0:T(8,128)(2,1)S(1)}, bf16[256,1152]{1,0:T(8,128)(2,1)S(1)}, u32[]{:S(2)}, u32[]{:S(2)}) collective-permute-start(bf16[256,1152]{1,0:T(8,128)(2,1)S(1)} %collective-permute-done.1.i1_ref), channel_id=1, source_target_pairs={{0,64},{1,961},{2,962},{3,67},{4,964},{5,69},{6,70},{7,967},{8,72}... | collective-permute-start | bytes 1769480 | tf_op jit(solution)/shard_map/ppermute | solution.py:35
  127.5 94.2 %collective-permute-start.3 = (bf16[264,1152]{1,0:T(8,128)(2,1)}, bf16[264,1152]{1,0:T(8,128)(2,1)S(1)}, u32[]{:S(2)}, u32[]{:S(2)}) collective-permute-start(bf16[264,1152]{1,0:T(8,128)(2,1)} %image_share.1), channel_id=1, source_target_pairs={{0,16},{1,1009},{2,1010},{3,19},{4,1012},{5,21},{6,22},{7,1015},{8... | collective-permute-start | bytes 1824776 | tf_op jit(solution)/shard_map/ppermute | solution.py:35
  148.3 15.6 %copy-start.1 = (bf16[256,1152]{1,0:T(8,128)(2,1)S(1)}, bf16[256,1152]{1,0:T(8,128)(2,1)}, u32[]{:S(2)}) copy-start(bf16[256,1152]{1,0:T(8,128)(2,1)} %i0_ref.3) | copy-start | bytes 1769476
  148.3 15.6 %copy-start.3 = (bf16[256,1152]{1,0:T(8,128)(2,1)S(1)}, bf16[256,1152]{1,0:T(8,128)(2,1)}, u32[]{:S(2)}) copy-start(bf16[256,1152]{1,0:T(8,128)(2,1)} %t0_ref.3) | copy-start | bytes 1769476
  151.1 97.1 %collective-permute-start.5 = (bf16[256,1152]{1,0:T(8,128)(2,1)}, bf16[256,1152]{1,0:T(8,128)(2,1)}, u32[]{:S(2)}, u32[]{:S(2)}) collective-permute-start(bf16[256,1152]{1,0:T(8,128)(2,1)} %text_share.1), channel_id=1, source_target_pairs={{0,1008},{1,17},{2,18},{3,1011},{4,20},{5,1013},{6,1014},{7,23},{8... | collective-permute-start | bytes 1769480 | tf_op jit(solution)/shard_map/ppermute | solution.py:35

commit v6 on v5

--- a/solution.py
+++ b/solution.py
@@ -153,22 +153,17 @@
 
 
 def sum_kernel(gi0, gt0, gi, gt, grad_image, grad_text):
-    grad_image[...] = (gi0[...] + gi[...].astype(jnp.float32)).astype(jnp.bfloat16)
+    grad_image[...] = (gi0[...] + gi[: gi0.shape[0], :].astype(jnp.float32)).astype(jnp.bfloat16)
     grad_text[...] = (gt0[...] + gt[...].astype(jnp.float32)).astype(jnp.bfloat16)
 
 
-def call(kernel, name, outs, flops, *args, steps=1):
+def call(kernel, name, outs, flops, *args):
     def spec(array):
-        if array.ndim == 1:
-            return pl.BlockSpec(memory_space=pltpu.SMEM)
-        if steps == 1:
-            return pl.BlockSpec(memory_space=pltpu.VMEM)
-        return pl.BlockSpec((outs[0].shape[0] // steps, array.shape[1]), lambda i: (i, 0))
+        return pl.BlockSpec(memory_space=pltpu.SMEM if array.ndim == 1 else pltpu.VMEM)
 
     return pl.pallas_call(
         kernel,
         name=name,
-        grid=(steps,) if steps > 1 else (),
         out_shape=outs,
         in_specs=[spec(a) for a in args],
         out_specs=[spec(a) for a in outs],
@@ -214,7 +209,7 @@
         scalars, image_embed, text_embed, i1_hat, t1_hat,
     )
     grad_image, grad_text = call(
-        sum_kernel, "total", [half, half], 4 * rows * wide, gi0, gt0, gi, gt, steps=4
+        sum_kernel, "total", [half, half], 4 * rows * wide, gi0, gt0, gi, gt
     )
     lines = gi[rows : rows + PIECES, :rows].astype(jnp.float32)
     return (loss0.reshape(rows) + jnp.sum(lines, axis=0), grad_image, grad_text)

time: 252 us -> 251 us (level)
  no operation moved by 1% of the time
where the time goes in v6:
time: 251 us; the launch traced here: 250 us
  waiting for transfers between devices  160 us (64%)
  starting transfers between devices  71.8 us (29%)
  Pallas kernels  14 us (6%)
    ppermute x6, waiting for transfers between devices, move(): return lax.ppermute(block, ('blk', 'grp'), route)  160 us
    ppermute x6, starting transfers between devices, move(): return lax.ppermute(block, ('blk', 'grp'), route)  71.8 us
    pallas_call x6, Pallas kernels, call(): pl.pallas_call(kernel, name=name, out_shape=outs, in_specs=[spec(a) for a...  14 us
  transfers between devices with their start and end apart: 6, of which 4 were waited for; matrix products, arithmetic and copies ran while one was open for 0% of the time, Pallas kernels for 5%

profile of v6, /device:TPU:33, one launch (start us, length us, event | category | flops | bytes accessed | tf_op | source)
XLA Modules:
  0.0 250.4 jit_solution(12577339171304560635)
XLA Ops:
  0.6 26.5 %collective-permute-start = (bf16[256,1152]{1,0:T(8,128)(2,1)}, bf16[256,1152]{1,0:T(8,128)(2,1)S(1)}, u32[]{:S(2)}, u32[]{:S(2)}) collective-permute-start(bf16[256,1152]{1,0:T(8,128)(2,1)} %t0_ref.3), channel_id=1, source_target_pairs={{0,1008},{1,17},{2,18},{3,1011},{4,20},{5,1013},{6,1014},{7,23},{8... | collective-permute-start | bytes 1769480 | tf_op jit(solution)/shard_map/ppermute | solution.py:35
  27.1 3.5 %collective-permute-start.1 = (bf16[256,1152]{1,0:T(8,128)(2,1)}, bf16[256,1152]{1,0:T(8,128)(2,1)S(1)}, u32[]{:S(2)}, u32[]{:S(2)}) collective-permute-start(bf16[256,1152]{1,0:T(8,128)(2,1)} %i0_ref.3), channel_id=1, source_target_pairs={{0,16},{1,1009},{2,1010},{3,19},{4,1012},{5,21},{6,22},{7,1015},{8... | collective-permute-start | bytes 1769480 | tf_op jit(solution)/shard_map/ppermute | solution.py:35
  32.0 0.0 copy-start
  32.0 1.1 copy-done
  33.0 0.0 copy-start.2
  33.0 1.1 copy-done.2
  34.1 0.4 own.1
  34.5 0.1 pad_maximum_fusion.scalars
  34.5 76.7 %collective-permute-done.t1_ref = bf16[256,1152]{1,0:T(8,128)(2,1)S(1)} collective-permute-done((bf16[256,1152]{1,0:T(8,128)(2,1)}, bf16[256,1152]{1,0:T(8,128)(2,1)S(1)}, u32[]{:S(2)}, u32[]{:S(2)}) %collective-permute-start) | collective-permute-done | bytes 589856 | tf_op jit(solution)/shard_map/ppermute | solution.py:35
  111.3 6.2 %collective-permute-start.2 = (bf16[256,1152]{1,0:T(8,128)(2,1)S(1)}, bf16[256,1152]{1,0:T(8,128)(2,1)S(1)}, u32[]{:S(2)}, u32[]{:S(2)}) collective-permute-start(bf16[256,1152]{1,0:T(8,128)(2,1)S(1)} %collective-permute-done.t1_ref), channel_id=1, source_target_pairs={{0,960},{1,65},{2,66},{3,963},{4,68},{5,965},{6,966},{7,71},{8,968... | collective-permute-start | bytes 1769480 | tf_op jit(solution)/shard_map/ppermute | solution.py:35
  117.5 0.0 collective-permute-done.1.i1_ref
  117.5 1.9 collective-permute-start.4
  119.4 2.8 %main.1 = (bf16[256,1152]{1,0:T(8,128)(2,1)S(1)}, bf16[256,1152]{1,0:T(8,128)(2,1)S(1)}, f32[256,1]{1,0:T(8,128)S(1)}, f32[256,1]{1,0:T(8,128)S(1)}, f32[256,115...) custom-call(f32[2]{0:T(128)S(1)} %pad_maximum_fusion.scalars, ...), custom_call_target="tpu_custom_call" | custom-call | flops 1056964608 | bytes 4194304 | tf_op jit(solution)/shard_map/main/pallas_call | solution.py:164
  122.3 2.0 collective-permute-done.2.tr_ref
  124.3 3.1 %image_share.1 = bf16[264,1152]{1,0:T(8,128)(2,1)} custom-call(f32[2]{0:T(128)S(1)} %pad_maximum_fusion.scalars, bf16[256,1152]{1,0:T(8,128)(2,1)S(1)} %collective-permute-done.1.i1_ref, bf16[256,1152]{1,0:T(8,128)(2,1)S(1)} %get-tuple-element.30.i1_hat, f32[256,1]{1,0:T(8,128)S(1)} %get-tuple-element.27.inv_i, ...), custom_call_target="tpu_custom_call" | custom-call | flops 301989888 | bytes 4194304 | tf_op jit(solution)/shard_map/image_share/pallas_call | solution.py:164
  127.5 20.8 %collective-permute-start.3 = (bf16[264,1152]{1,0:T(8,128)(2,1)}, bf16[264,1152]{1,0:T(8,128)(2,1)S(1)}, u32[]{:S(2)}, u32[]{:S(2)}) collective-permute-start(bf16[264,1152]{1,0:T(8,128)(2,1)} %image_share.1), channel_id=1, source_target_pairs={{0,16},{1,1009},{2,1010},{3,19},{4,1012},{5,21},{6,22},{7,1015},{8... | collective-permute-start | bytes 1824776 | tf_op jit(solution)/shard_map/ppermute | solution.py:35
  148.3 0.0 collective-permute-done.4.ir_ref
  148.3 0.0 copy-start.1
  148.3 0.0 copy-start.3
  148.3 2.7 %text_share.1 = bf16[256,1152]{1,0:T(8,128)(2,1)} custom-call(f32[2]{0:T(128)S(1)} %pad_maximum_fusion.scalars, bf16[256,1152]{1,0:T(8,128)(2,1)S(1)} %collective-permute-done.t1_ref, bf16[256,1152]{1,0:T(8,128)(2,1)S(1)} %get-tuple-element.31.t1_hat, f32[256,1]{1,0:T(8,128)S(1)} %get-tuple-element.35.inv_t, ...), custom_call_target="tpu_custom_call" | custom-call | flops 301989888 | bytes 4194304 | tf_op jit(solution)/shard_map/text_share/pallas_call | solution.py:164
  151.1 12.8 %collective-permute-start.5 = (bf16[256,1152]{1,0:T(8,128)(2,1)}, bf16[256,1152]{1,0:T(8,128)(2,1)}, u32[]{:S(2)}, u32[]{:S(2)}) collective-permute-start(bf16[256,1152]{1,0:T(8,128)(2,1)} %text_share.1), channel_id=1, source_target_pairs={{0,1008},{1,17},{2,18},{3,1011},{4,20},{5,1013},{6,1014},{7,23},{8... | collective-permute-start | bytes 1769480 | tf_op jit(solution)/shard_map/ppermute | solution.py:35
  163.9 0.0 copy-done.1
  163.9 0.0 copy-done.3
  164.0 2.7 %home.1 = (f32[256,1152]{1,0:T(8,128)S(1)}, f32[256,1152]{1,0:T(8,128)S(1)}, f32[256,1]{1,0:T(8,128)S(1)}) custom-call(f32[2]{0:T(128)S(1)} %pad_maximum_fusion.scalars, bf16[256,1152]{1,0:T(8,128)(2,1)S(1)} %copy-done.1, bf16[256,1152]{1,0:T(8,128)(2,1)S(1)} %copy-done.3, bf16[256,1152]{1,0:T(8,128)(2,1)S(1)} %get-tuple-element.30.i1_hat, ...), custom_call_target="tpu_custom_call" | custom-call | flops 1056964608 | bytes 4194304 | tf_op jit(solution)/shard_map/home/pallas_call | solution.py:164
  166.7 0.1 reduce
  166.8 54.9 %collective-permute-done.3.gi = bf16[264,1152]{1,0:T(8,128)(2,1)S(1)} collective-permute-done((bf16[264,1152]{1,0:T(8,128)(2,1)}, bf16[264,1152]{1,0:T(8,128)(2,1)S(1)}, u32[]{:S(2)}, u32[]{:S(2)}) %collective-permute-start.3) | collective-permute-done | bytes 608288 | tf_op jit(solution)/shard_map/ppermute | solution.py:35
  221.7 0.6 add.3
  222.3 26.0 %collective-permute-done.5.gt = bf16[256,1152]{1,0:T(8,128)(2,1)} collective-permute-done((bf16[256,1152]{1,0:T(8,128)(2,1)}, bf16[256,1152]{1,0:T(8,128)(2,1)}, u32[]{:S(2)}, u32[]{:S(2)}) %collective-permute-start.5) | collective-permute-done | bytes 589856 | tf_op jit(solution)/shard_map/ppermute | solution.py:35
  248.2 2.2 total.1
  (1 shorter events, 0.0 us)
Async XLA Ops:
  0.6 110.6 %collective-permute-start = (bf16[256,1152]{1,0:T(8,128)(2,1)}, bf16[256,1152]{1,0:T(8,128)(2,1)S(1)}, u32[]{:S(2)}, u32[]{:S(2)}) collective-permute-start(bf16[256,1152]{1,0:T(8,128)(2,1)} %t0_ref.3), channel_id=1, source_target_pairs={{0,1008},{1,17},{2,18},{3,1011},{4,20},{5,1013},{6,1014},{7,23},{8... | collective-permute-start | bytes 1769480 | tf_op jit(solution)/shard_map/ppermute | solution.py:35
  27.1 90.4 %collective-permute-start.1 = (bf16[256,1152]{1,0:T(8,128)(2,1)}, bf16[256,1152]{1,0:T(8,128)(2,1)S(1)}, u32[]{:S(2)}, u32[]{:S(2)}) collective-permute-start(bf16[256,1152]{1,0:T(8,128)(2,1)} %i0_ref.3), channel_id=1, source_target_pairs={{0,16},{1,1009},{2,1010},{3,19},{4,1012},{5,21},{6,22},{7,1015},{8... | collective-permute-start | bytes 1769480 | tf_op jit(solution)/shard_map/ppermute | solution.py:35
  32.0 1.1 copy-start
  33.0 1.1 copy-start.2
  111.3 13.0 %collective-permute-start.2 = (bf16[256,1152]{1,0:T(8,128)(2,1)S(1)}, bf16[256,1152]{1,0:T(8,128)(2,1)S(1)}, u32[]{:S(2)}, u32[]{:S(2)}) collective-permute-start(bf16[256,1152]{1,0:T(8,128)(2,1)S(1)} %collective-permute-done.t1_ref), channel_id=1, source_target_pairs={{0,960},{1,65},{2,66},{3,963},{4,68},{5,965},{6,966},{7,71},{8,968... | collective-permute-start | bytes 1769480 | tf_op jit(solution)/shard_map/ppermute | solution.py:35
  117.5 30.8 %collective-permute-start.4 = (bf16[256,1152]{1,0:T(8,128)(2,1)S(1)}, bf16[256,1152]{1,0:T(8,128)(2,1)S(1)}, u32[]{:S(2)}, u32[]{:S(2)}) collective-permute-start(bf16[256,1152]{1,0:T(8,128)(2,1)S(1)} %collective-permute-done.1.i1_ref), channel_id=1, source_target_pairs={{0,64},{1,961},{2,962},{3,67},{4,964},{5,69},{6,70},{7,967},{8,72}... | collective-permute-start | bytes 1769480 | tf_op jit(solution)/shard_map/ppermute | solution.py:35
  127.5 94.2 %collective-permute-start.3 = (bf16[264,1152]{1,0:T(8,128)(2,1)}, bf16[264,1152]{1,0:T(8,128)(2,1)S(1)}, u32[]{:S(2)}, u32[]{:S(2)}) collective-permute-start(bf16[264,1152]{1,0:T(8,128)(2,1)} %image_share.1), channel_id=1, source_target_pairs={{0,16},{1,1009},{2,1010},{3,19},{4,1012},{5,21},{6,22},{7,1015},{8... | collective-permute-start | bytes 1824776 | tf_op jit(solution)/shard_map/ppermute | solution.py:35
  148.3 15.6 %copy-start.1 = (bf16[256,1152]{1,0:T(8,128)(2,1)S(1)}, bf16[256,1152]{1,0:T(8,128)(2,1)}, u32[]{:S(2)}) copy-start(bf16[256,1152]{1,0:T(8,128)(2,1)} %i0_ref.3) | copy-start | bytes 1769476
  148.3 15.6 %copy-start.3 = (bf16[256,1152]{1,0:T(8,128)(2,1)S(1)}, bf16[256,1152]{1,0:T(8,128)(2,1)}, u32[]{:S(2)}) copy-start(bf16[256,1152]{1,0:T(8,128)(2,1)} %t0_ref.3) | copy-start | bytes 1769476
  151.1 97.1 %collective-permute-start.5 = (bf16[256,1152]{1,0:T(8,128)(2,1)}, bf16[256,1152]{1,0:T(8,128)(2,1)}, u32[]{:S(2)}, u32[]{:S(2)}) collective-permute-start(bf16[256,1152]{1,0:T(8,128)(2,1)} %text_share.1), channel_id=1, source_target_pairs={{0,1008},{1,17},{2,18},{3,1011},{4,20},{5,1013},{6,1014},{7,23},{8... | collective-permute-start | bytes 1769480 | tf_op jit(solution)/shard_map/ppermute | solution.py:35

commit v7 on v6

--- a/solution.py
+++ b/solution.py
@@ -95,26 +95,28 @@
 
 
 def main_kernel(
-    scalars, i0_hat, t0_hat, i1_ref, t1_ref, i1_hat, t1_hat, inv_i, inv_t, di1, dt1, loss1
+    scalars, t0_hat, i1_ref, t1_ref, i1_hat, t1_hat, inv_i, inv_t, w11_ref, di1, loss1
 ):
     inv_i[...], _, i1 = normalize(i1_ref)
     inv_t[...], _, t1 = normalize(t1_ref)
     i1_hat[...] = i1
     t1_hat[...] = t1
-    i0, t0 = i0_hat[...], t0_hat[...]
-    _, w01 = pair_of(scalars, i0, t1)
+    t0 = t0_hat[...]
     a, w11 = pair_of(scalars, i1, t1)
-    dt1[...] = dot_tn(w01, i0) + dot_tn(w11, i1)
+    w11_ref[...] = w11
     b, w10 = pair_of(scalars, i1, t0)
     loss1[...] = a + b
     di1[...] = dot_nn(w10, t0) + dot_nn(w11, t1)
 
 
-def text_kernel(scalars, t1_ref, t1_hat, inv_t, ir_ref, dt1, gt1):
+def text_kernel(scalars, t1_ref, t1_hat, inv_t, ir_ref, i0_hat, i1_hat, w11, gt1):
     _, _, ir = normalize(ir_ref)
-    _, weights = pair_of(scalars, ir, t1_hat[...])
+    i0, t1 = i0_hat[...], t1_hat[...]
+    _, weights = pair_of(scalars, ir, t1)
+    _, w01 = pair_of(scalars, i0, t1)
+    total = dot_tn(w01, i0) + dot_tn(w11[...], i1_hat[...]) + dot_tn(weights, ir)
     unit = t1_ref[...].astype(jnp.float32) * inv_t[...]
-    grad = scalars[0] * (dt1[...] + dot_tn(weights, ir))
+    grad = scalars[0] * total
     gt1[...] = project(inv_t[...], unit, grad).astype(jnp.bfloat16)
 
 
@@ -179,6 +181,7 @@
     scalars = jnp.concatenate([jnp.exp(log_temp), logit_bias])
     full = jax.ShapeDtypeStruct((rows, wide), jnp.float32)
     half = jax.ShapeDtypeStruct((rows, wide), jnp.bfloat16)
+    square = jax.ShapeDtypeStruct((rows, rows), jnp.bfloat16)
     column = jax.ShapeDtypeStruct((rows, 1), jnp.float32)
     product = 2 * rows * rows * wide
 
@@ -188,13 +191,13 @@
     t1, i0_hat, scalars = lax.optimization_barrier((t1, i0_hat, scalars))
     ir = pass_image(i1)
     tr = pass_text(t1)
-    i1_hat, t1_hat, inv_i, inv_t, di1, dt1, loss1 = call(
-        main_kernel, "main", [half, half, column, column, full, full, column], 7 * product,
-        scalars, i0_hat, t0_hat, i1, t1,
+    i1_hat, t1_hat, inv_i, inv_t, w11, di1, loss1 = call(
+        main_kernel, "main", [half, half, column, column, square, full, column], 4 * product,
+        scalars, t0_hat, i1, t1,
     )
     (gt1,) = call(
-        text_kernel, "text_share", [half], 2 * product,
-        scalars, t1, t1_hat, inv_t, ir, dt1,
+        text_kernel, "text_share", [half], 5 * product,
+        scalars, t1, t1_hat, inv_t, ir, i0_hat, i1_hat, w11,
     )
     gt = swap_text(gt1)
     taller = jax.ShapeDtypeStruct((rows + EXTRA, wide), jnp.bfloat16)

time: 251 us -> 251 us (level)
  transfers between devices with their start and end apart: 6 -> 6, of which waited for: 4 -> 4; matrix products, arithmetic and copies ran while one was open for 0% -> 0% of each run, Pallas kernels for 5% -> 4%
where the time goes in v7:
time: 251 us; the launch traced here: 250 us
  waiting for transfers between devices  161 us (64%)
  starting transfers between devices  71.1 us (28%)
  Pallas kernels  13.2 us (5%)
    ppermute x6, waiting for transfers between devices, move(): return lax.ppermute(block, ('blk', 'grp'), route)  161 us
    ppermute x6, starting transfers between devices, move(): return lax.ppermute(block, ('blk', 'grp'), route)  71.1 us
    pallas_call x6, Pallas kernels, call(): pl.pallas_call(kernel, name=name, out_shape=outs, in_specs=[spec(a) for a...  13.2 us
  transfers between devices with their start and end apart: 6, of which 4 were waited for; matrix products, arithmetic and copies ran while one was open for 0% of the time, Pallas kernels for 4%

profile of v7, /device:TPU:33, one launch (start us, length us, event | category | flops | bytes accessed | tf_op | source)
XLA Modules:
  0.0 250.4 jit_solution(17233115028269915052)
XLA Ops:
  0.6 26.5 %collective-permute-start = (bf16[256,1152]{1,0:T(8,128)(2,1)}, bf16[256,1152]{1,0:T(8,128)(2,1)S(1)}, u32[]{:S(2)}, u32[]{:S(2)}) collective-permute-start(bf16[256,1152]{1,0:T(8,128)(2,1)} %t0_ref.3), channel_id=1, source_target_pairs={{0,1008},{1,17},{2,18},{3,1011},{4,20},{5,1013},{6,1014},{7,23},{8... | collective-permute-start | bytes 1769480 | tf_op jit(solution)/shard_map/ppermute | solution.py:35
  27.1 3.5 %collective-permute-start.1 = (bf16[256,1152]{1,0:T(8,128)(2,1)}, bf16[256,1152]{1,0:T(8,128)(2,1)S(1)}, u32[]{:S(2)}, u32[]{:S(2)}) collective-permute-start(bf16[256,1152]{1,0:T(8,128)(2,1)} %i0_ref.3), channel_id=1, source_target_pairs={{0,16},{1,1009},{2,1010},{3,19},{4,1012},{5,21},{6,22},{7,1015},{8... | collective-permute-start | bytes 1769480 | tf_op jit(solution)/shard_map/ppermute | solution.py:35
  32.0 0.0 copy-start
  32.0 1.1 copy-done
  33.0 0.0 copy-start.2
  33.0 1.1 copy-done.2
  34.1 0.4 own.1
  34.5 0.1 pad_maximum_fusion.scalars
  34.5 76.7 %collective-permute-done.t1_ref = bf16[256,1152]{1,0:T(8,128)(2,1)S(1)} collective-permute-done((bf16[256,1152]{1,0:T(8,128)(2,1)}, bf16[256,1152]{1,0:T(8,128)(2,1)S(1)}, u32[]{:S(2)}, u32[]{:S(2)}) %collective-permute-start) | collective-permute-done | bytes 589856 | tf_op jit(solution)/shard_map/ppermute | solution.py:35
  111.3 6.2 %collective-permute-start.2 = (bf16[256,1152]{1,0:T(8,128)(2,1)S(1)}, bf16[256,1152]{1,0:T(8,128)(2,1)S(1)}, u32[]{:S(2)}, u32[]{:S(2)}) collective-permute-start(bf16[256,1152]{1,0:T(8,128)(2,1)S(1)} %collective-permute-done.t1_ref), channel_id=1, source_target_pairs={{0,960},{1,65},{2,66},{3,963},{4,68},{5,965},{6,966},{7,71},{8,968... | collective-permute-start | bytes 1769480 | tf_op jit(solution)/shard_map/ppermute | solution.py:35
  117.5 0.0 collective-permute-done.1.i1_ref
  117.5 1.9 collective-permute-start.4
  119.4 2.0 main.1
  121.5 2.8 %collective-permute-done.2.tr_ref = bf16[256,1152]{1,0:T(8,128)(2,1)S(1)} collective-permute-done((bf16[256,1152]{1,0:T(8,128)(2,1)S(1)}, bf16[256,1152]{1,0:T(8,128)(2,1)S(1)}, u32[]{:S(2)}, u32[]{:S(2)}) %collective-permute-start.2) | collective-permute-done | bytes 589856 | tf_op jit(solution)/shard_map/ppermute | solution.py:35
  124.3 3.1 %image_share.1 = bf16[264,1152]{1,0:T(8,128)(2,1)} custom-call(f32[2]{0:T(128)S(1)} %pad_maximum_fusion.scalars, bf16[256,1152]{1,0:T(8,128)(2,1)S(1)} %collective-permute-done.1.i1_ref, bf16[256,1152]{1,0:T(8,128)(2,1)S(1)} %get-tuple-element.29.i1_hat, f32[256,1]{1,0:T(8,128)S(1)} %get-tuple-element.26.inv_i, ...), custom_call_target="tpu_custom_call" | custom-call | flops 301989888 | bytes 4194304 | tf_op jit(solution)/shard_map/image_share/pallas_call | solution.py:166
  127.5 20.8 %collective-permute-start.3 = (bf16[264,1152]{1,0:T(8,128)(2,1)}, bf16[264,1152]{1,0:T(8,128)(2,1)S(1)}, u32[]{:S(2)}, u32[]{:S(2)}) collective-permute-start(bf16[264,1152]{1,0:T(8,128)(2,1)} %image_share.1), channel_id=1, source_target_pairs={{0,16},{1,1009},{2,1010},{3,19},{4,1012},{5,21},{6,22},{7,1015},{8... | collective-permute-start | bytes 1824776 | tf_op jit(solution)/shard_map/ppermute | solution.py:35
  148.3 0.0 collective-permute-done.4.ir_ref
  148.3 0.0 copy-start.1
  148.3 0.0 copy-start.3
  148.3 2.8 %text_share.1 = bf16[256,1152]{1,0:T(8,128)(2,1)} custom-call(f32[2]{0:T(128)S(1)} %pad_maximum_fusion.scalars, bf16[256,1152]{1,0:T(8,128)(2,1)S(1)} %collective-permute-done.t1_ref, bf16[256,1152]{1,0:T(8,128)(2,1)S(1)} %get-tuple-element.30.t1_hat, f32[256,1]{1,0:T(8,128)S(1)} %get-tuple-element.34.inv_t, ...), custom_call_target="tpu_custom_call" | custom-call | flops 754974720 | bytes 4194304 | tf_op jit(solution)/shard_map/text_share/pallas_call | solution.py:166
  151.2 12.1 %collective-permute-start.5 = (bf16[256,1152]{1,0:T(8,128)(2,1)}, bf16[256,1152]{1,0:T(8,128)(2,1)}, u32[]{:S(2)}, u32[]{:S(2)}) collective-permute-start(bf16[256,1152]{1,0:T(8,128)(2,1)} %text_share.1), channel_id=1, source_target_pairs={{0,1008},{1,17},{2,18},{3,1011},{4,20},{5,1013},{6,1014},{7,23},{8... | collective-permute-start | bytes 1769480 | tf_op jit(solution)/shard_map/ppermute | solution.py:35
  163.3 0.0 copy-done.1
  163.3 0.0 copy-done.3
  163.3 2.7 %home.1 = (f32[256,1152]{1,0:T(8,128)S(1)}, f32[256,1152]{1,0:T(8,128)S(1)}, f32[256,1]{1,0:T(8,128)S(1)}) custom-call(f32[2]{0:T(128)S(1)} %pad_maximum_fusion.scalars, bf16[256,1152]{1,0:T(8,128)(2,1)S(1)} %copy-done.1, bf16[256,1152]{1,0:T(8,128)(2,1)S(1)} %copy-done.3, bf16[256,1152]{1,0:T(8,128)(2,1)S(1)} %get-tuple-element.29.i1_hat, ...), custom_call_target="tpu_custom_call" | custom-call | flops 1056964608 | bytes 4194304 | tf_op jit(solution)/shard_map/home/pallas_call | solution.py:166
  166.0 0.1 reduce
  166.1 56.2 %collective-permute-done.3.gi = bf16[264,1152]{1,0:T(8,128)(2,1)S(1)} collective-permute-done((bf16[264,1152]{1,0:T(8,128)(2,1)}, bf16[264,1152]{1,0:T(8,128)(2,1)S(1)}, u32[]{:S(2)}, u32[]{:S(2)}) %collective-permute-start.3) | collective-permute-done | bytes 608288 | tf_op jit(solution)/shard_map/ppermute | solution.py:35
  222.4 0.6 add.3
  222.9 25.3 %collective-permute-done.5.gt = bf16[256,1152]{1,0:T(8,128)(2,1)} collective-permute-done((bf16[256,1152]{1,0:T(8,128)(2,1)}, bf16[256,1152]{1,0:T(8,128)(2,1)}, u32[]{:S(2)}, u32[]{:S(2)}) %collective-permute-start.5) | collective-permute-done | bytes 589856 | tf_op jit(solution)/shard_map/ppermute | solution.py:35
  248.2 2.2 total.1
  (1 shorter events, 0.0 us)
Async XLA Ops:
  0.6 110.6 %collective-permute-start = (bf16[256,1152]{1,0:T(8,128)(2,1)}, bf16[256,1152]{1,0:T(8,128)(2,1)S(1)}, u32[]{:S(2)}, u32[]{:S(2)}) collective-permute-start(bf16[256,1152]{1,0:T(8,128)(2,1)} %t0_ref.3), channel_id=1, source_target_pairs={{0,1008},{1,17},{2,18},{3,1011},{4,20},{5,1013},{6,1014},{7,23},{8... | collective-permute-start | bytes 1769480 | tf_op jit(solution)/shard_map/ppermute | solution.py:35
  27.1 90.4 %collective-permute-start.1 = (bf16[256,1152]{1,0:T(8,128)(2,1)}, bf16[256,1152]{1,0:T(8,128)(2,1)S(1)}, u32[]{:S(2)}, u32[]{:S(2)}) collective-permute-start(bf16[256,1152]{1,0:T(8,128)(2,1)} %i0_ref.3), channel_id=1, source_target_pairs={{0,16},{1,1009},{2,1010},{3,19},{4,1012},{5,21},{6,22},{7,1015},{8... | collective-permute-start | bytes 1769480 | tf_op jit(solution)/shard_map/ppermute | solution.py:35
  32.0 1.1 copy-start
  33.0 1.1 copy-start.2
  111.3 13.0 %collective-permute-start.2 = (bf16[256,1152]{1,0:T(8,128)(2,1)S(1)}, bf16[256,1152]{1,0:T(8,128)(2,1)S(1)}, u32[]{:S(2)}, u32[]{:S(2)}) collective-permute-start(bf16[256,1152]{1,0:T(8,128)(2,1)S(1)} %collective-permute-done.t1_ref), channel_id=1, source_target_pairs={{0,960},{1,65},{2,66},{3,963},{4,68},{5,965},{6,966},{7,71},{8,968... | collective-permute-start | bytes 1769480 | tf_op jit(solution)/shard_map/ppermute | solution.py:35
  117.5 30.8 %collective-permute-start.4 = (bf16[256,1152]{1,0:T(8,128)(2,1)S(1)}, bf16[256,1152]{1,0:T(8,128)(2,1)S(1)}, u32[]{:S(2)}, u32[]{:S(2)}) collective-permute-start(bf16[256,1152]{1,0:T(8,128)(2,1)S(1)} %collective-permute-done.1.i1_ref), channel_id=1, source_target_pairs={{0,64},{1,961},{2,962},{3,67},{4,964},{5,69},{6,70},{7,967},{8,72}... | collective-permute-start | bytes 1769480 | tf_op jit(solution)/shard_map/ppermute | solution.py:35
  127.5 94.9 %collective-permute-start.3 = (bf16[264,1152]{1,0:T(8,128)(2,1)}, bf16[264,1152]{1,0:T(8,128)(2,1)S(1)}, u32[]{:S(2)}, u32[]{:S(2)}) collective-permute-start(bf16[264,1152]{1,0:T(8,128)(2,1)} %image_share.1), channel_id=1, source_target_pairs={{0,16},{1,1009},{2,1010},{3,19},{4,1012},{5,21},{6,22},{7,1015},{8... | collective-permute-start | bytes 1824776 | tf_op jit(solution)/shard_map/ppermute | solution.py:35
  148.3 15.0 %copy-start.1 = (bf16[256,1152]{1,0:T(8,128)(2,1)S(1)}, bf16[256,1152]{1,0:T(8,128)(2,1)}, u32[]{:S(2)}) copy-start(bf16[256,1152]{1,0:T(8,128)(2,1)} %i0_ref.3) | copy-start | bytes 1769476
  148.3 15.0 %copy-start.3 = (bf16[256,1152]{1,0:T(8,128)(2,1)S(1)}, bf16[256,1152]{1,0:T(8,128)(2,1)}, u32[]{:S(2)}) copy-start(bf16[256,1152]{1,0:T(8,128)(2,1)} %t0_ref.3) | copy-start | bytes 1769476
  151.2 97.0 %collective-permute-start.5 = (bf16[256,1152]{1,0:T(8,128)(2,1)}, bf16[256,1152]{1,0:T(8,128)(2,1)}, u32[]{:S(2)}, u32[]{:S(2)}) collective-permute-start(bf16[256,1152]{1,0:T(8,128)(2,1)} %text_share.1), channel_id=1, source_target_pairs={{0,1008},{1,17},{2,18},{3,1011},{4,20},{5,1013},{6,1014},{7,23},{8... | collective-permute-start | bytes 1769480 | tf_op jit(solution)/shard_map/ppermute | solution.py:35
